TPU v7x, 128 devices: a whole 4x4x4 slice. The times are simulated.
128 devices in a mesh: dp: 16 (over y_hi, z, core), tensor: 8 (over x, y_lo).
Axes of the slice: x: 4, y: 4 (y_hi: 2, y_lo: 2; y = y_hi * 2 + y_lo), z: 4, core: 2. Of those that a mesh axis runs over, the one named last changes fastest.
Arguments:
- x_rows: bfloat16 [3072, 16384], P(('dp', 'tensor')), may hold values from -6 to 6
- w_key: bfloat16 [16384, 512], P('dp', 'tensor'), may hold values from -0.046875 to 0.046875
- w_value: bfloat16 [16384, 512], P('dp', 'tensor'), may hold values from -0.046875 to 0.046875
- w_query: bfloat16 [16384, 8192], P('dp', 'tensor'), may hold values from -0.046875 to 0.046875
- queries: bfloat16 [3072, 8192], P('dp', 'tensor'), may hold values from -4 to 4
- grad_out: bfloat16 [3072, 8192], P('dp', 'tensor'), may hold values from -6 to 6
- segment_ids: int32 [16, 192], P('dp'), may hold values from 0 to 7, never falling along the last dimension, each value on 1 to 96 neighbouring positions
Outputs:
- grad_queries: bfloat16 [3072, 8192], P('dp', 'tensor')
- grad_rows: bfloat16 [3072, 16384], P(('dp', 'tensor'))
- grad_key_weight: float32 [16384, 512], P('dp', 'tensor')
- grad_value_weight: float32 [16384, 512], P('dp', 'tensor')
- grad_query_weight: float32 [16384, 8192], P('dp', 'tensor')
Inputs may be any that keep to these rules, and one draw needn't show every extreme that they name: `segment_ids`: in each rollout batch the document numbers never fall, each of the 8 documents holds 1 to 96 tokens, and one holds exactly 96.
All inputs are finite; a program needn't handle non-finite values.
Results may differ from a plain program's by a relative error of at most 0.038.
Values may be sent and summed in bfloat16 or wider, within the bound.
A program may use at most 128 MiB of HBM per device.

v0:
```python
import jax
import jax.numpy as jnp
from jax import lax
from jax.sharding import PartitionSpec as P

theta_base = 500000.0


def partner(block, axis, distance):
    count = lax.axis_size(axis)
    route = []
    for low in range(count):
        high = low | 1 << distance
        if high != low and high < count:
            route += [(low, high), (high, low)]
    return lax.ppermute(block, axis, route)


def rotary_tables(segment_row, head_dim):
    count = segment_row.shape[0]
    places = jnp.arange(count, dtype=jnp.int32)
    earlier = jnp.concatenate([segment_row[:1] - 1, segment_row[:-1]])
    starts = lax.cummax(jnp.where(segment_row != earlier, places, 0), axis=0)
    position = (places - starts).astype(jnp.float32)
    half = head_dim // 2
    freqs = theta_base ** (-(2.0 * jnp.arange(half, dtype=jnp.float32)) / head_dim)
    angles = position[:, None] * freqs[None, :]
    allowed = (segment_row[:, None] == segment_row[None, :]) & (places[None, :] <= places[:, None])
    return (jnp.cos(angles), jnp.sin(angles), allowed)


def shards(x_rows, w_key, w_value, w_query, queries, grad_out, segment_ids):
    half = w_key.shape[1]
    head_dim = 2 * half
    tokens = queries.shape[0]
    heads = queries.shape[1] // head_dim
    scale = 1.0 / head_dim**0.5
    lower_half = lax.axis_index("tensor") % 2 == 0
    cosine, sine, allowed = rotary_tables(segment_ids[0], head_dim)
    whole_batch = lax.all_gather(x_rows, "tensor", axis=0, tiled=True)
    columns = lax.all_to_all(whole_batch, "dp", split_axis=1, concat_axis=0, tiled=True)
    joined = jnp.concatenate([w_key, w_value], axis=1)
    own_lin = lax.psum_scatter(
        jnp.dot(columns, joined, preferred_element_type=jnp.float32).astype(jnp.bfloat16),
        "dp",
        scatter_dimension=0,
        tiled=True,
    )
    partner_lin = partner(own_lin, "tensor", 0)
    first = jnp.where(lower_half, own_lin, partner_lin)
    second = jnp.where(lower_half, partner_lin, own_lin)
    key_first = first[:, :half]
    key_second = second[:, :half]
    values = jnp.concatenate([first[:, half:], second[:, half:]], axis=1)
    first_f = key_first.astype(jnp.float32)
    second_f = key_second.astype(jnp.float32)
    keys = jnp.concatenate(
        [first_f * cosine - second_f * sine, second_f * cosine + first_f * sine], axis=1
    ).astype(jnp.bfloat16)
    query_heads = queries.reshape(tokens, heads, head_dim)
    dout_heads = grad_out.reshape(tokens, heads, head_dim)
    scores = (
        jnp.einsum("thd,sd->hts", query_heads, keys, preferred_element_type=jnp.float32) * scale
    )
    weights = jnp.where(allowed[None], jnp.exp(scores), 0.0)
    probs = weights / jnp.sum(weights, axis=-1, keepdims=True)
    dprob = jnp.einsum("thd,sd->hts", dout_heads, values, preferred_element_type=jnp.float32)
    delta = jnp.sum(probs * dprob, axis=-1, keepdims=True)
    dscore = (probs * (dprob - delta)).astype(jnp.bfloat16)
    probs_low = probs.astype(jnp.bfloat16)
    grad_q = jnp.einsum("hts,sd->thd", dscore, keys, preferred_element_type=jnp.float32) * scale
    grad_queries = grad_q.astype(jnp.bfloat16).reshape(tokens, heads * head_dim)
    key_part = (
        jnp.einsum("hts,thd->sd", dscore, query_heads, preferred_element_type=jnp.float32) * scale
    )
    value_part = jnp.einsum(
        "hts,thd->sd", probs_low, dout_heads, preferred_element_type=jnp.float32
    )
    other_keyg, other_valueg = (
        partner(key_part.astype(jnp.bfloat16), "tensor", 0).astype(key_part.dtype),
        partner(value_part.astype(jnp.bfloat16), "tensor", 0).astype(value_part.dtype),
    )
    key_rot = key_part + other_keyg
    value_sum = value_part + other_valueg
    upper = key_rot[:, :half]
    lower = key_rot[:, half:]
    grad_key_lin = jnp.concatenate(
        [upper * cosine + lower * sine, lower * cosine - upper * sine], axis=1
    ).astype(jnp.bfloat16)
    grad_value = value_sum.astype(jnp.bfloat16)
    own_key = jnp.where(lower_half, grad_key_lin[:, :half], grad_key_lin[:, half:])
    own_value = jnp.where(lower_half, grad_value[:, :half], grad_value[:, half:])
    own_grad = jnp.concatenate([own_key, own_value], axis=1)
    all_query, all_own = (
        lax.all_gather(grad_queries, "dp", axis=0, tiled=True),
        lax.all_gather(own_grad, "dp", axis=0, tiled=True),
    )
    contract_rows = (((0,), (0,)), ((), ()))
    contract_cols = (((1,), (1,)), ((), ()))
    pair_weight = lax.dot_general(
        columns, all_own, contract_rows, preferred_element_type=jnp.float32
    )
    query_weight = lax.dot_general(
        columns, all_query, contract_rows, preferred_element_type=jnp.float32
    )
    term = lax.dot_general(all_query, w_query, contract_cols, preferred_element_type=jnp.float32)
    term = term + lax.dot_general(
        all_own, joined, contract_cols, preferred_element_type=jnp.float32
    )
    returned = lax.all_to_all(
        term.astype(jnp.bfloat16), "dp", split_axis=0, concat_axis=1, tiled=True
    )
    grad_rows = lax.psum_scatter(
        returned.astype(jnp.float32).astype(jnp.bfloat16), "tensor", scatter_dimension=0, tiled=True
    )
    return (grad_queries, grad_rows, pair_weight[:, :half], pair_weight[:, half:], query_weight)


def solution(mesh):
    placed = (
        P(("dp", "tensor"), None),
        P("dp", "tensor"),
        P("dp", "tensor"),
        P("dp", "tensor"),
        P("dp", "tensor"),
        P("dp", "tensor"),
        P("dp", None),
    )
    return jax.shard_map(
        shards,
        mesh=mesh,
        in_specs=placed,
        out_specs=(
            P("dp", "tensor"),
            P(("dp", "tensor"), None),
            P("dp", "tensor"),
            P("dp", "tensor"),
            P("dp", "tensor"),
        ),
        check_vma=False,
    )
```

profile of v0, /device:TPU:1, one launch (start us, length us, event | category | flops | bytes accessed | tf_op | source)
XLA Modules:
  0.0 628.7 jit_solution(3018946577277951397)
XLA Ops:
  7.2 0.7 all-gather.3.cloned.1.call-update
  7.9 134.0 %all-gather.3.cloned.1.call-done = bf16[192,16384]{1,0:T(8,128)(2,1)} async-done(((bf16[24,16384]{1,0:T(8,128)(2,1)}), bf16[192,16384]{1,0:T(8,128)(2,1)}) %all-gather.3.cloned.1.call-update) | async-done | bytes 6291472 | tf_op jit(solution)/shard_map/all_gather | solution.py:40
  141.9 6.5 %copy.98 = bf16[24,16,8,1024]{3,2,0,1:T(8,128)(2,1)} copy(bf16[24,16,8,1024]{3,2,1,0:T(8,128)(2,1)} %bitcast.107) | data formatting | bytes 12582912 | tf_op jit(solution)/shard_map/all_to_all | solution.py:41
  148.4 7.4 %all-to-all-start = ((bf16[192,16,1024]{2,0,1:T(8,128)(2,1)}), bf16[192,16,1024]{2,0,1:T(8,128)(2,1)}, u32[]{:S(2)}, u32[]{:S(2)}) async-start(bf16[192,16,1024]{2,0,1:T(8,128)(2,1)} %bitcast.104), calls=%async_computation | async-start | bytes 12582912 | tf_op jit(solution)/shard_map/all_to_all | solution.py:41
  155.8 0.0 reduce-scatter.7.cloned.1.call-start
  155.9 86.2 %all-to-all-done = bf16[192,16,1024]{2,0,1:T(8,128)(2,1)} async-done(((bf16[192,16,1024]{2,0,1:T(8,128)(2,1)}), bf16[192,16,1024]{2,0,1:T(8,128)(2,1)}, u32[]{:S(2)}, u32[]{:S(2)}) %all-to-all-start) | async-done | bytes 6291488 | tf_op jit(solution)/shard_map/all_to_all | solution.py:41
  242.1 5.0 fusion
  247.2 1.2 copy.67
  248.3 0.0 all-gather.5.cloned.1.call-start
  248.4 0.5 slice.57
  249.6 0.1 compare_select_fusion
  249.6 0.3 reduce-window.9
  250.0 0.1 slice.60
  250.1 0.1 slice_reduce_fusion
  250.2 0.1 maximum_bitcast_fusion.5
  250.3 0.1 fusion.19
  250.4 70.9 %reduce-scatter.7.cloned.1.call-done = bf16[192,128]{1,0:T(8,128)(2,1)} async-done(((bf16[3072,128]{1,0:T(8,128)(2,1)}), bf16[192,128]{1,0:T(8,128)(2,1)}) %reduce-scatter.7.cloned.1.call-update) | async-done | bytes 49168 | tf_op jit(solution)/shard_map/reduce_scatter | solution.py:43
  321.3 0.5 collective-permute-start
  321.8 2.7 collective-permute-done
  324.4 0.8 broadcast_select_fusion.1
  325.2 0.1 slice.76
  325.3 0.1 slice.77
  325.4 0.5 fusion.29
  325.9 1.6 fusion.11
  327.5 3.5 fusion.1
  330.9 2.1 fusion.3
  333.1 1.4 fusion.5
  334.4 0.9 copy.99
  335.3 0.0 reduce-scatter.5.cloned.1.call-start
  335.4 1.8 fusion.43
  337.1 0.6 collective-permute-start.2
  337.7 1.4 fusion.44
  339.1 1.1 collective-permute-start.1
  340.2 0.1 slice_select_fusion
  340.3 1.8 collective-permute-done.1
  342.1 0.5 fusion.36
  342.6 0.1 pad_maximum_fusion
  342.7 30.0 %all_gather.11 = bf16[3072,128]{1,0:T(8,128)(2,1)S(1)} all-gather(bf16[192,128]{1,0:T(8,128)(2,1)S(1)} %pad_maximum_fusion), channel_id=1, replica_groups=mesh['dp'=16,'tensor'=8] {'dp'}, dimensions={0}, use_global_device_ids=true | all-gather | bytes 835584 | tf_op jit(solution)/shard_map/all_gather | solution.py:96
  372.6 31.5 %all-gather.5.cloned.1.call-done = bf16[3072,1024]{1,0:T(8,128)(2,1)} async-done(((bf16[192,1024]{1,0:T(8,128)(2,1)}), bf16[3072,1024]{1,0:T(8,128)(2,1)}) %all-gather.5.cloned.1.call-update) | async-done | bytes 6291472 | tf_op jit(solution)/shard_map/all_gather | solution.py:95
  404.1 9.0 %fusion.47 = f32[3072,1024]{1,0:T(8,128)S(1)} fusion(bf16[3072,1024]{1,0:T(8,128)(2,1)} %all-gather.5.cloned.1.call-done, bf16[1024,1024]{1,0:T(8,128)(2,1)S(1)} %copy-done), kind=kOutput, calls=%fused_computation.76 | convolution fusion | flops 6442450944 | bytes 20971520 | tf_op jit(solution)/shard_map/dot_general | solution.py:106
  413.1 1.8 add_convert_fusion
  414.9 75.9 %all_to_all.38 = bf16[16,192,1024]{2,1,0:T(8,128)(2,1)S(1)} all-to-all(bf16[16,192,1024]{2,1,0:T(8,128)(2,1)S(1)} %bitcast.105), channel_id=1, replica_groups=mesh['dp'=16,'tensor'=8] {'dp'}, dimensions={0} | all-to-all | bytes 12582912 | tf_op jit(solution)/shard_map/all_to_all | solution.py:110
  490.8 3.4 copy.73
  494.2 3.8 convolution_bitcast_fusion.1
  498.0 0.8 fusion.42
  498.9 12.8 %convolution_bitcast_fusion = f32[1024,1024]{0,1:T(8,128)} fusion(bf16[3072,1024]{1,0:T(8,128)(2,1)} %all-gather.5.cloned.1.call-done, bf16[3072,1024]{1,0:T(8,128)(2,1)} %bitcast.1), kind=kOutput, calls=%fused_computation.4 | convolution fusion | flops 6442450944 | bytes 16777216 | tf_op jit(solution)/shard_map/dot_general | solution.py:103
  511.7 5.3 copy.65
  517.0 105.2 %reduce-scatter.5.cloned.1.call-done = bf16[24,16384]{1,0:T(8,128)(2,1)} async-done(((bf16[192,16384]{1,0:T(8,128)(2,1)}), bf16[24,16384]{1,0:T(8,128)(2,1)}) %reduce-scatter.5.cloned.1.call-update) | async-done | bytes 786448 | tf_op jit(solution)/shard_map/reduce_scatter | solution.py:113
  (29 shorter events, 0.3 us)
Async XLA Ops:
  7.2 396.9 %copy-start = (bf16[1024,1024]{1,0:T(8,128)(2,1)S(1)}, bf16[1024,1024]{1,0:T(8,128)(2,1)}, u32[]{:S(2)}) copy-start(bf16[1024,1024]{1,0:T(8,128)(2,1)} %param.10) | copy-start | bytes 6291460
  7.2 134.7 %all-gather.3.cloned.1.call-start = ((), (), s32[]{:S(2)}) async-start(), calls=%async_computation.4 | async-start | bytes 7077888 | tf_op jit(solution)/shard_map/all_gather | solution.py:40
  148.4 7.5 %copy-start.5 = (bf16[1024,64]{0,1:T(8,128)(2,1)S(1)}, bf16[1024,64]{0,1:T(8,128)(2,1)}, u32[]{:S(2)}) copy-start(bf16[1024,64]{0,1:T(8,128)(2,1)} %param.8) | copy-start | bytes 393220
  148.4 7.5 %copy-start.6 = (bf16[1024,64]{0,1:T(8,128)(2,1)S(1)}, bf16[1024,64]{0,1:T(8,128)(2,1)}, u32[]{:S(2)}) copy-start(bf16[1024,64]{0,1:T(8,128)(2,1)} %param.9) | copy-start | bytes 393220
  148.4 93.7 %all-to-all-start = ((bf16[192,16,1024]{2,0,1:T(8,128)(2,1)}), bf16[192,16,1024]{2,0,1:T(8,128)(2,1)}, u32[]{:S(2)}, u32[]{:S(2)}) async-start(bf16[192,16,1024]{2,0,1:T(8,128)(2,1)} %bitcast.104), calls=%async_computation | async-start | bytes 12582912 | tf_op jit(solution)/shard_map/all_to_all | solution.py:41
  155.8 165.5 %reduce-scatter.7.cloned.1.call-start = ((), (), s32[]{:S(2)}) async-start(), calls=%async_computation.7 | async-start | bytes 835584 | tf_op jit(solution)/shard_map/reduce_scatter | solution.py:43
  242.1 6.3 copy-start.7
  242.1 83.7 %copy-start.2 = (bf16[192,1024]{1,0:T(8,128)(2,1)S(1)}, bf16[192,1024]{1,0:T(8,128)(2,1)}, u32[]{:S(2)}) copy-start(bf16[192,1024]{1,0:T(8,128)(2,1)} %param.12) | copy-start | bytes 1179652
  248.3 155.8 %all-gather.5.cloned.1.call-start = ((), (), s32[]{:S(2)}) async-start(), calls=%async_computation.5 | async-start | bytes 6684672 | tf_op jit(solution)/shard_map/all_gather | solution.py:95
  321.3 3.2 collective-permute-start
  325.9 5.0 copy-start.3
  325.9 5.0 copy-start.4
  335.3 286.9 %reduce-scatter.5.cloned.1.call-start = ((), (), s32[]{:S(2)}) async-start(), calls=%async_computation.6 | async-start | bytes 7077888 | tf_op jit(solution)/shard_map/reduce_scatter | solution.py:113
  337.1 3.0 collective-permute-start.2
  339.1 3.0 collective-permute-start.1
  498.9 123.4 %copy-start.1 = (bf16[1024,1024]{1,0:T(8,128)(2,1)S(1)}, bf16[1024,1024]{1,0:T(8,128)(2,1)}, u32[]{:S(2)}) copy-start(bf16[1024,1024]{1,0:T(8,128)(2,1)} %param.10) | copy-start | bytes 6291460
Sparse Core Ops, SparseCore 0:
  9.7 132.2 all-gather.2
  248.5 72.7 reduce-scatter.6
  335.4 68.6 all-gather.4
  494.3 127.8 reduce-scatter.4
where the time goes:
time: 629 us
  waiting for transfers between devices  433 us (69%)
  blocking collectives  106 us (17%)
  matrix products  41.9 us (7%)
  local copies, waits for them, and re-layouts  18.9 us (3%)
  between operations  14.6 us (2%)
  starting transfers between devices  9.71 us (2%)
    all_gather x1, waiting for transfers between devices, shards(): whole_batch = lax.all_gather(x_rows, 'tensor', axis=0, tiled=True)  134 us
    reduce_scatter x1, waiting for transfers between devices, shards(): lax.psum_scatter(returned.astype(jnp.float32).astype(jnp.bfloat16), 'tens...  105 us
    all_to_all x1, waiting for transfers between devices, shards(): lax.all_to_all(whole_batch, 'dp', split_axis=1, concat_axis=0, tiled=True)  86.2 us
    all_to_all x1, blocking collectives, shards(): lax.all_to_all(term.astype(jnp.bfloat16), 'dp', split_axis=0, concat_axis...  75.9 us
    reduce_scatter x1, waiting for transfers between devices, shards(): lax.psum_scatter(jnp.dot(columns, joined, preferred_element_type=jnp.floa...  70.9 us
    all_gather x1, waiting for transfers between devices, shards(): lax.all_gather(grad_queries, 'dp', axis=0, tiled=True)  31.5 us
    all_gather x1, blocking collectives, shards(): lax.all_gather(own_grad, 'dp', axis=0, tiled=True)  30 us
    dot_general x1, matrix products, shards(): lax.dot_general(columns, all_query, contract_rows, preferred_element_type...  12.8 us
  transfers between devices with their start and end apart: 8, of which 7 were waited for; matrix products, arithmetic and copies ran while one was open for 4% of the time, Pallas kernels for 0%

commit v1 on v0

--- a/solution.py
+++ b/solution.py
@@ -37,8 +37,14 @@
     scale = 1.0 / head_dim**0.5
     lower_half = lax.axis_index("tensor") % 2 == 0
     cosine, sine, allowed = rotary_tables(segment_ids[0], head_dim)
-    whole_batch = lax.all_gather(x_rows, "tensor", axis=0, tiled=True)
-    columns = lax.all_to_all(whole_batch, "dp", split_axis=1, concat_axis=0, tiled=True)
+    own_rows = x_rows.shape[0]
+    batches = lax.axis_size("dp")
+    groups = lax.axis_size("tensor")
+    own_tokens = lax.all_to_all(x_rows, "dp", split_axis=1, concat_axis=0, tiled=True)
+    features = own_tokens.shape[1]
+    columns = lax.all_gather(own_tokens, "tensor", axis=0, tiled=False)
+    columns = columns.reshape(groups, batches, own_rows, features).transpose(1, 0, 2, 3)
+    columns = columns.reshape(batches * tokens, features)
     joined = jnp.concatenate([w_key, w_value], axis=1)
     own_lin = lax.psum_scatter(
         jnp.dot(columns, joined, preferred_element_type=jnp.float32).astype(jnp.bfloat16),
@@ -107,12 +113,10 @@
     term = term + lax.dot_general(
         all_own, joined, contract_cols, preferred_element_type=jnp.float32
     )
-    returned = lax.all_to_all(
-        term.astype(jnp.bfloat16), "dp", split_axis=0, concat_axis=1, tiled=True
-    )
-    grad_rows = lax.psum_scatter(
-        returned.astype(jnp.float32).astype(jnp.bfloat16), "tensor", scatter_dimension=0, tiled=True
-    )
+    by_owner = term.astype(jnp.bfloat16).reshape(batches, groups, own_rows, features)
+    by_owner = by_owner.transpose(1, 0, 2, 3).reshape(groups * batches * own_rows, features)
+    reduced = lax.psum_scatter(by_owner, "tensor", scatter_dimension=0, tiled=True)
+    grad_rows = lax.all_to_all(reduced, "dp", split_axis=0, concat_axis=1, tiled=True)
     return (grad_queries, grad_rows, pair_weight[:, :half], pair_weight[:, half:], query_weight)
 
 

time: 629 us -> 499 us (0.79)
  waiting for transfers between devices: 433 us -> 348 us
  blocking collectives: 106 us -> 53.7 us
    all_to_all x1, waiting for transfers between devices: 86.2 us -> 0.01 us  [shards(): lax.all_to_all(reduced, 'dp', split_axis=0, concat_axis=1, tiled=True)]
    all_to_all x1, blocking collectives: 75.9 us -> 23.7 us  [shards(): lax.all_to_all(x_rows, 'dp', split_axis=1, concat_axis=0, tiled=True)]
    reduce_scatter x1, waiting for transfers between devices: 105 us -> 123 us  [shards(): lax.psum_scatter(by_owner, 'tensor', scatter_dimension=0, tiled=True)]
    all_gather x1, waiting for transfers between devices: 134 us -> 126 us  [shards(): columns = lax.all_gather(own_tokens, 'tensor', axis=0, tiled=False)]
    all_to_all x2, local copies, waits for them, and re-layouts: 9.82 us -> 2.28 us  [the longest x1 1.34 us: shards(): lax.all_to_all(x_rows, 'dp', split_axis=1, concat_axis=0, tiled=True)]
    reduce_scatter x1, waiting for transfers between devices: 70.9 us -> 63.9 us  [shards(): lax.psum_scatter(jnp.dot(columns, joined, preferred_element_type=jnp.floa...]
  transfers between devices with their start and end apart: 8 -> 8, of which waited for: 7 -> 6; matrix products, arithmetic and copies ran while one was open for 4% -> 6% of each run, Pallas kernels for 0% -> 0%
where the time goes in v1:
time: 499 us
  waiting for transfers between devices  348 us (70%)
  blocking collectives  53.7 us (11%)
  matrix products  46.4 us (9%)
  local copies, waits for them, and re-layouts  21.8 us (4%)
  between operations  14.6 us (3%)
  starting transfers between devices  9.44 us (2%)
    all_gather x1, waiting for transfers between devices, shards(): columns = lax.all_gather(own_tokens, 'tensor', axis=0, tiled=False)  126 us
    reduce_scatter x1, waiting for transfers between devices, shards(): lax.psum_scatter(by_owner, 'tensor', scatter_dimension=0, tiled=True)  123 us
    reduce_scatter x1, waiting for transfers between devices, shards(): lax.psum_scatter(jnp.dot(columns, joined, preferred_element_type=jnp.floa...  63.9 us
    all_gather x1, waiting for transfers between devices, shards(): lax.all_gather(grad_queries, 'dp', axis=0, tiled=True)  31.4 us
    all_gather x1, blocking collectives, shards(): lax.all_gather(own_grad, 'dp', axis=0, tiled=True)  30.1 us
    all_to_all x1, blocking collectives, shards(): lax.all_to_all(x_rows, 'dp', split_axis=1, concat_axis=0, tiled=True)  23.7 us
    dot_general x1, matrix products, shards(): lax.dot_general(all_query, w_query, contract_cols, preferred_element_type...  12.4 us
    dot_general x1, matrix products, shards(): lax.dot_general(columns, all_query, contract_rows, preferred_element_type...  12.1 us
  transfers between devices with their start and end apart: 8, of which 6 were waited for; matrix products, arithmetic and copies ran while one was open for 6% of the time, Pallas kernels for 0%

profile of v1, /device:TPU:1, one launch (start us, length us, event | category | flops | bytes accessed | tf_op | source)
XLA Modules:
  0.0 498.5 jit_solution(4423228879122285574)
XLA Ops:
  7.2 1.3 copy.115
  8.6 23.7 %all_to_all.35 = bf16[24,16,1024]{2,0,1:T(8,128)(2,1)} all-to-all(bf16[24,16,1024]{2,0,1:T(8,128)(2,1)S(1)} %bitcast.119), channel_id=1, replica_groups=mesh['dp'=16,'tensor'=8] {'dp'}, dimensions={1} | all-to-all | bytes 1572864 | tf_op jit(solution)/shard_map/all_to_all | solution.py:43
  32.3 0.0 reduce-scatter.7.cloned.1.call-start
  32.3 0.9 constant_dynamic-update-slice_fusion.1
  33.3 125.6 %all-gather.3.cloned.1.call-done = bf16[8,384,1024]{2,1,0:T(8,128)(2,1)} async-done(((bf16[1,384,1024]{2,1,0:T(8,128)(2,1)}), bf16[8,384,1024]{2,1,0:T(8,128)(2,1)}) %all-gather.3.cloned.1.call-update) | async-done | bytes 6291472 | tf_op jit(solution)/shard_map/all_gather | solution.py:45
  158.8 3.5 copy.70
  162.4 2.6 copy-done.2
  164.9 2.2 fusion
  167.1 1.2 copy.84
  168.4 0.5 slice.57
  169.5 0.1 compare_select_fusion
  169.6 0.3 reduce-window.9
  169.9 0.1 slice.60
  170.1 0.1 slice_reduce_fusion
  170.2 0.1 maximum_bitcast_fusion.5
  170.3 0.1 fusion.19
  170.4 63.9 %reduce-scatter.7.cloned.1.call-done = bf16[192,128]{1,0:T(8,128)(2,1)} async-done(((bf16[3072,128]{1,0:T(8,128)(2,1)}), bf16[192,128]{1,0:T(8,128)(2,1)}) %reduce-scatter.7.cloned.1.call-update) | async-done | bytes 49168 | tf_op jit(solution)/shard_map/reduce_scatter | solution.py:49
  234.3 0.5 collective-permute-start
  234.7 2.7 collective-permute-done
  237.4 0.8 broadcast_select_fusion.1
  238.2 0.1 slice.76
  238.3 0.1 slice.77
  238.4 0.5 fusion.29
  238.9 1.6 fusion.11
  240.5 3.4 fusion.1
  243.9 2.1 fusion.3
  246.0 1.4 fusion.5
  247.4 0.9 copy.116
  248.3 1.8 fusion.43
  250.1 0.5 collective-permute-start.2
  250.6 1.4 fusion.44
  252.0 1.1 collective-permute-start.1
  253.1 0.1 slice_select_fusion
  253.2 1.8 collective-permute-done.1
  255.0 0.5 fusion.36
  255.5 0.1 pad_maximum_fusion
  255.6 30.1 %all_gather.15 = bf16[3072,128]{1,0:T(8,128)(2,1)S(1)} all-gather(bf16[192,128]{1,0:T(8,128)(2,1)S(1)} %pad_maximum_fusion), channel_id=1, replica_groups=mesh['dp'=16,'tensor'=8] {'dp'}, dimensions={0}, use_global_device_ids=true | all-gather | bytes 835584 | tf_op jit(solution)/shard_map/all_gather | solution.py:102
  285.7 31.4 %all-gather.5.cloned.1.call-done = bf16[3072,1024]{1,0:T(8,128)(2,1)} async-done(((bf16[192,1024]{1,0:T(8,128)(2,1)}), bf16[3072,1024]{1,0:T(8,128)(2,1)}) %all-gather.5.cloned.1.call-update) | async-done | bytes 6291472 | tf_op jit(solution)/shard_map/all_gather | solution.py:101
  317.1 12.4 %fusion.47 = f32[3072,1024]{1,0:T(8,128)} fusion(bf16[3072,1024]{1,0:T(8,128)(2,1)} %all-gather.5.cloned.1.call-done, bf16[1024,1024]{1,0:T(8,128)(2,1)S(1)} %copy-done), kind=kOutput, calls=%fused_computation.76 | convolution fusion | flops 6442450944 | bytes 20971520 | tf_op jit(solution)/shard_map/dot_general | solution.py:112
  329.5 6.4 %add_convert_fusion = bf16[3072,1024]{1,0:T(8,128)(2,1)S(1)} fusion(f32[3072,1024]{1,0:T(8,128)} %fusion.47, bf16[3072,128]{1,0:T(8,128)(2,1)S(1)} %all_gather.15, bf16[1024,128]{0,1:T(8,128)(2,1)S(1)} %constant_dynamic-update-slice_fusion), kind=kOutput, calls=%fused_computation | convolution fusion | flops 811597824 | bytes 19922944 | tf_op jit(solution)/shard_map/dot_general | solution.py:113
  335.8 3.4 copy.80
  339.2 3.8 convolution_bitcast_fusion.1
  343.0 0.8 fusion.42
  343.9 122.5 %reduce-scatter.5.cloned.1.call-done = bf16[384,1024]{1,0:T(8,128)(2,1)} async-done(((bf16[3072,1024]{1,0:T(8,128)(2,1)}), bf16[384,1024]{1,0:T(8,128)(2,1)}) %reduce-scatter.5.cloned.1.call-update) | async-done | bytes 786448 | tf_op jit(solution)/shard_map/reduce_scatter | solution.py:118
  466.4 7.2 %all-to-all-start.1 = ((bf16[16,24,1024]{2,1,0:T(8,128)(2,1)}), bf16[16,24,1024]{2,1,0:T(8,128)(2,1)S(1)}, u32[]{:S(2)}, u32[]{:S(2)}) async-start(bf16[16,24,1024]{2,1,0:T(8,128)(2,1)} %bitcast.123), calls=%async_computation.2 | async-start | bytes 1572864 | tf_op jit(solution)/shard_map/all_to_all | solution.py:119
  473.6 12.1 %convolution_bitcast_fusion = f32[1024,1024]{0,1:T(8,128)} fusion(bf16[3072,1024]{1,0:T(8,128)(2,1)} %all-gather.5.cloned.1.call-done, bf16[3072,1024]{1,0:T(8,128)(2,1)} %bitcast.113), kind=kOutput, calls=%fused_computation.3 | convolution fusion | flops 6442450944 | bytes 16777216 | tf_op jit(solution)/shard_map/dot_general | solution.py:109
  485.7 5.3 %copy.82 = f32[1024,1024]{1,0:T(8,128)} copy(f32[1024,1024]{0,1:T(8,128)} %convolution_bitcast_fusion) | data formatting | bytes 8388608
  491.1 0.9 copy.90
  (31 shorter events, 0.4 us)
Async XLA Ops:
  7.2 309.9 %copy-start = (bf16[1024,1024]{1,0:T(8,128)(2,1)S(1)}, bf16[1024,1024]{1,0:T(8,128)(2,1)}, u32[]{:S(2)}) copy-start(bf16[1024,1024]{1,0:T(8,128)(2,1)} %param.10) | copy-start | bytes 6291460
  7.2 26.0 %copy-start.6 = (bf16[1024,64]{0,1:T(8,128)(2,1)S(1)}, bf16[1024,64]{0,1:T(8,128)(2,1)}, u32[]{:S(2)}) copy-start(bf16[1024,64]{0,1:T(8,128)(2,1)} %param.9) | copy-start | bytes 393220
  7.2 151.7 %all-gather.3.cloned.1.call-start = ((), (), s32[]{:S(2)}) async-start(), calls=%async_computation.4 | async-start | bytes 7077888 | tf_op jit(solution)/shard_map/all_gather | solution.py:45
  32.3 202.0 %reduce-scatter.7.cloned.1.call-start = ((), (), s32[]{:S(2)}) async-start(), calls=%async_computation.7 | async-start | bytes 835584 | tf_op jit(solution)/shard_map/reduce_scatter | solution.py:49
  162.3 2.6 copy-start.2
  164.9 3.4 copy-start.7
  164.9 73.9 %copy-start.3 = (bf16[192,1024]{1,0:T(8,128)(2,1)S(1)}, bf16[192,1024]{1,0:T(8,128)(2,1)}, u32[]{:S(2)}) copy-start(bf16[192,1024]{1,0:T(8,128)(2,1)} %param.12) | copy-start | bytes 1179652
  168.3 148.7 %all-gather.5.cloned.1.call-start = ((), (), s32[]{:S(2)}) async-start(), calls=%async_computation.5 | async-start | bytes 6684672 | tf_op jit(solution)/shard_map/all_gather | solution.py:101
  234.3 3.2 collective-permute-start
  238.9 5.0 %copy-start.4 = (bf16[192,64]{1,0:T(8,128)(2,1)}, bf16[192,64]{1,0:T(8,128)(2,1)S(1)}, u32[]{:S(2)}) copy-start(bf16[192,64]{1,0:T(8,128)(2,1)S(1)} %get-tuple-element.32) | copy-start | bytes 73732
  238.9 5.0 %copy-start.5 = (bf16[192,64]{1,0:T(8,128)(2,1)}, bf16[192,64]{1,0:T(8,128)(2,1)S(1)}, u32[]{:S(2)}) copy-start(bf16[192,64]{1,0:T(8,128)(2,1)S(1)} %get-tuple-element.33) | copy-start | bytes 73732
  248.3 218.1 %reduce-scatter.5.cloned.1.call-start = ((), (), s32[]{:S(2)}) async-start(), calls=%async_computation.6 | async-start | bytes 7077888 | tf_op jit(solution)/shard_map/reduce_scatter | solution.py:118
  250.1 3.0 collective-permute-start.2
  252.0 3.0 collective-permute-start.1
  466.4 24.7 %all-to-all-start.1 = ((bf16[16,24,1024]{2,1,0:T(8,128)(2,1)}), bf16[16,24,1024]{2,1,0:T(8,128)(2,1)S(1)}, u32[]{:S(2)}, u32[]{:S(2)}) async-start(bf16[16,24,1024]{2,1,0:T(8,128)(2,1)} %bitcast.123), calls=%async_computation.2 | async-start | bytes 1572864 | tf_op jit(solution)/shard_map/all_to_all | solution.py:119
  473.6 18.4 %copy-start.1 = (bf16[1024,1024]{1,0:T(8,128)(2,1)S(1)}, bf16[1024,1024]{1,0:T(8,128)(2,1)}, u32[]{:S(2)}) copy-start(bf16[1024,1024]{1,0:T(8,128)(2,1)} %param.10) | copy-start | bytes 6291460
Sparse Core Ops, SparseCore 0:
  32.4 126.4 all-gather.2
  168.4 65.7 reduce-scatter.6
  248.4 68.6 all-gather.4
  339.4 126.9 reduce-scatter.4

commit v2 on v0

v2 whole, which is shorter than its diff:
```python
import functools

import jax
import jax.numpy as jnp
import numpy as np
from jax import lax
from jax.experimental import pallas as pl
from jax.experimental.pallas import tpu as pltpu
from jax.sharding import PartitionSpec as P

theta_base = 500000.0
MESH = pl.DeviceIdType.MESH
F32 = jnp.float32
BF16 = jnp.bfloat16

N_DP = 16
N_T = 8
ROWS = 24
TOK = 192
FEAT = 1024
COLS = 1024
HD = 128
HALF = 64
WIDE = COLS + HD
SLOTS = (0, 2, 6, 8, 10, 14, 4, 12)
ORDERS = ((1, 2, 6), (2, 6, 1), (6, 1, 2))


def xor_ring(place, mask):
    if mask == 0:
        return place
    if mask == 1:
        return place + 1 - 2 * lax.rem(place, 2)
    if mask == 2:
        return lax.rem(place + 2, 4)
    return 3 - place


def xor_dp(d, mask):
    y_hi, z, core = d // 8, lax.rem(d // 2, 4), lax.rem(d, 2)
    y_hi = 1 - y_hi if mask & 8 else y_hi
    core = 1 - core if mask & 1 else core
    return y_hi * 8 + xor_ring(z, (mask // 2) % 4) * 2 + core


def xor_t(t, mask):
    x, y_lo = t // 2, lax.rem(t, 2)
    y_lo = 1 - y_lo if mask & 1 else y_lo
    return xor_ring(x, mask // 2) * 2 + y_lo


def rows_at(start, size, unit):
    return pl.ds(pl.multiple_of(start, unit), size)


def remote(src, dst, send, recv, d, t):
    return pltpu.make_async_remote_copy(
        src_ref=src, dst_ref=dst, send_sem=send, recv_sem=recv, device_id=(d, t), device_id_type=MESH
    )


def fold(block):
    return jnp.concatenate([block[:, : FEAT // 2], block[:, FEAT // 2 :]], axis=0)


def unfold(block):
    return jnp.concatenate([block[:ROWS], block[ROWS:]], axis=1)


def dot_nt(a, b):
    return lax.dot_general(a, b, (((1,), (1,)), ((), ())), preferred_element_type=F32)


def dot_nn(a, b):
    return lax.dot_general(a, b, (((1,), (0,)), ((), ())), preferred_element_type=F32)


def dot_tn(a, b):
    return lax.dot_general(a, b, (((0,), (0,)), ((), ())), preferred_element_type=F32)


class Gather:
    def __init__(self, buf, slot_rows, chunks, send, recv, d, t):
        self.buf, self.slot_rows, self.chunks = buf, slot_rows, chunks
        self.send, self.recv, self.d, self.t = send, recv, d, t

    def copies(self, stage, arriving):
        out = []
        for c, (offset, size) in enumerate(self.chunks):
            first, second, third = ORDERS[c]
            held = ([0], [0, first], [0, first, second, first ^ second])[stage]
            link = ORDERS[c][stage]
            for j in held:
                slot = xor_t(self.t, j ^ link if arriving else j)
                part = self.buf.at[rows_at(slot * self.slot_rows + offset, size, 16)]
                n = (j ^ link) - 1
                out.append(
                    remote(part, part, self.send.at[c, n], self.recv.at[c, n], self.d, xor_t(self.t, link))
                )
        return out

    def start(self, stage):
        for copy in self.copies(stage, False):
            copy.start()

    def wait(self, stage):
        for copy in self.copies(stage, True):
            copy.wait_recv()

    def finish(self):
        for stage in range(3):
            for copy in self.copies(stage, False):
                copy.wait_send()


def front(
    x_ref, wk_ref, wv_ref, q_ref, do_ref, seg_ref, freq_ref,
    gq_ref, own_ref, xg,
    xsend, xa, wg, kvf, kvsend, kvrecv, heads_out, heads_in, part_out, part_in,
    cos_ref, sin_ref, mask_ref, keyp, valuep, key_ref, value_ref,
    x_s, x_r, w_s, w_r, g_s, g_r, kv_s, kv_r, h_s, h_r, p_s, p_r,
):
    d = lax.axis_index("dp")
    t = lax.axis_index("tensor")
    barrier = pltpu.get_barrier_semaphore()

    def greet_dp(k, carry):
        pl.semaphore_signal(barrier, inc=1, device_id=(lax.rem(d + k, N_DP), t), device_id_type=MESH)
        return carry

    def greet_t(k, carry):
        pl.semaphore_signal(barrier, inc=1, device_id=(d, lax.rem(t + k, N_T)), device_id_type=MESH)
        return carry

    lax.fori_loop(1, N_DP, greet_dp, 0)
    lax.fori_loop(1, N_T, greet_t, 0)
    wg[rows_at(t * HD, HALF, HALF)] = wk_ref[...]
    wg[rows_at(t * HD + HALF, HALF, HALF)] = wv_ref[...]
    pl.semaphore_wait(barrier, N_DP + N_T - 2)

    weights = Gather(wg, HD, ((0, 48), (48, 48), (96, 32)), w_s, w_r, d, t)
    weights.start(0)

    def x_copy(k, to):
        return remote(xsend.at[to], xa.at[d], x_s.at[k], x_r.at[k], to, t)

    def pack_x(k, carry):
        to = lax.rem(d + k, N_DP)
        block = x_ref[:, rows_at(to * FEAT, FEAT, FEAT)].astype(F32)
        xsend[to] = fold(block).astype(BF16)
        x_copy(k, to).start()
        return carry

    lax.fori_loop(1, N_DP, pack_x, 0)
    xa[d] = fold(x_ref[:, rows_at(d * FEAT, FEAT, FEAT)].astype(F32)).astype(BF16)
    weights.wait(0)
    weights.start(1)

    row_no = lax.broadcasted_iota(jnp.int32, (TOK, TOK), 0)
    col_no = lax.broadcasted_iota(jnp.int32, (TOK, TOK), 1)
    seg_row = jnp.broadcast_to(seg_ref[...], (TOK, TOK))
    seg_col = jnp.sum(jnp.where(row_no == col_no, seg_row, 0), axis=1, keepdims=True)
    earlier = jnp.sum((seg_row < seg_col).astype(F32), axis=1, keepdims=True)
    place = lax.broadcasted_iota(jnp.int32, (TOK, 1), 0).astype(F32)
    angle = (place - earlier) * freq_ref[...]
    cos_ref[...] = jnp.cos(angle)
    sin_ref[...] = jnp.sin(angle)
    mask_ref[...] = ((seg_row == seg_col) & (col_no <= row_no)).astype(F32)

    weights.wait(1)
    weights.start(2)

    def wait_x(k, carry):
        x_copy(k, lax.rem(d + k, N_DP)).wait_send()
        remote(
            xsend.at[d], xa.at[lax.rem(d + N_DP - k, N_DP)], x_s.at[k], x_r.at[k], d, t
        ).wait_recv()
        return carry

    lax.fori_loop(1, N_DP, wait_x, 0)
    for s, mask in enumerate(SLOTS):
        pair = [unfold(xa[xor_dp(d, mask ^ e)].astype(F32)) for e in range(2)]
        xg[rows_at(t * (N_DP * ROWS) + s * 2 * ROWS, 2 * ROWS, 16)] = jnp.concatenate(pair, axis=0).astype(BF16)
    tokens = Gather(xg, N_DP * ROWS, ((0, 128), (128, 128), (256, 128)), g_s, g_r, d, t)
    tokens.start(0)

    weights.wait(2)

    def project(n, carry):
        own = xg[rows_at(t * (N_DP * ROWS), N_DP * ROWS, 16)]
        kvf[:, rows_at(n * 256, 256, 256)] = dot_nt(own, wg[rows_at(n * 256, 256, 256)])
        return carry

    lax.fori_loop(0, 4, project, 0)

    def kv_copy(mask, to, slot):
        return remote(kvsend.at[mask], kvrecv.at[slot], kv_s.at[mask], kv_r.at[mask], to, t)

    for s, base in enumerate(SLOTS):
        for e in range(2):
            mask = base ^ e
            block = fold(kvf[(2 * s + e) * ROWS : (2 * s + e + 1) * ROWS]).astype(BF16)
            if mask == 0:
                kvrecv[0] = block
            else:
                kvsend[mask] = block
                kv_copy(mask, xor_dp(d, mask), mask).start()
    tokens.wait(0)
    tokens.start(1)
    for mask in range(1, N_DP):
        kv_copy(mask, xor_dp(d, mask), mask).wait()

    def add_kv(k, total):
        return total + kvrecv[k].astype(F32)

    lin = lax.fori_loop(1, N_DP, add_kv, kvrecv[0].astype(F32))
    for head in range(4):
        rows = lin[(head // 2) * ROWS : (head // 2 + 1) * ROWS, (head % 2) * 256 : (head % 2 + 1) * 256]
        heads_out[head] = jnp.concatenate([rows[:, :HD], rows[:, HD:]], axis=0).astype(BF16)

    def head_copy(k, to):
        return remote(heads_out.at[to // 2], heads_in.at[t], h_s.at[k], h_r.at[k], d, to)

    def send_heads(k, carry):
        head_copy(k, lax.rem(t + k, N_T)).start()
        return carry

    lax.fori_loop(1, N_T, send_heads, 0)
    heads_in[t] = heads_out[t // 2]
    tokens.wait(1)
    tokens.start(2)

    def wait_heads(k, carry):
        head_copy(k, lax.rem(t + k, N_T)).wait_send()
        slot = lax.rem(t + N_T - k, N_T)
        remote(heads_out.at[0], heads_in.at[slot], h_s.at[k], h_r.at[k], d, slot).wait_recv()
        return carry

    lax.fori_loop(1, N_T, wait_heads, 0)
    blocks = [heads_in[i].astype(F32) for i in range(N_T)]
    first = jnp.concatenate([b[:ROWS] for b in blocks], axis=0)
    second = jnp.concatenate([b[ROWS:] for b in blocks], axis=0)
    cosine, sine = cos_ref[...], sin_ref[...]
    a, c = first[:, :HALF], second[:, :HALF]
    key_ref[...] = jnp.concatenate([a * cosine - c * sine, c * cosine + a * sine], axis=1).astype(BF16)
    value_ref[...] = jnp.concatenate([first[:, HALF:], second[:, HALF:]], axis=1).astype(BF16)
    keyp[...] = jnp.zeros_like(keyp)
    valuep[...] = jnp.zeros_like(valuep)
    scale = 1.0 / HD**0.5

    def head_step(h, carry):
        cols = rows_at(h * HD, HD, HD)
        q, do = q_ref[:, cols], do_ref[:, cols]
        key, value = key_ref[...], value_ref[...]
        allowed = mask_ref[...] > 0.0
        weight = jnp.where(allowed, jnp.exp(dot_nt(q, key) * scale), 0.0)
        probs = weight / jnp.sum(weight, axis=1, keepdims=True)
        dprob = dot_nt(do, value)
        delta = jnp.sum(probs * dprob, axis=1, keepdims=True)
        dscore = (probs * (dprob - delta)).astype(BF16)
        gq_ref[:, cols] = (dot_nn(dscore, key) * scale).astype(BF16)
        keyp[...] += dot_tn(dscore, q)
        valuep[...] += dot_tn(probs.astype(BF16), do)
        return carry

    lax.fori_loop(0, COLS // HD, head_step, 0)
    key_part = keyp[...] * scale
    part_out[0:TOK] = key_part.astype(BF16)
    part_out[TOK : 2 * TOK] = valuep[...].astype(BF16)
    part = remote(part_out, part_in, p_s, p_r, d, xor_t(t, 1))
    part.start()
    part.wait()
    key_rot = key_part + part_in[0:TOK].astype(F32)
    value_sum = valuep[...] + part_in[TOK : 2 * TOK].astype(F32)
    upper, lower = key_rot[:, :HALF], key_rot[:, HALF:]
    is_first = lax.rem(t, 2) == 0
    own_key = jnp.where(is_first, upper * cosine + lower * sine, lower * cosine - upper * sine)
    own_value = jnp.where(is_first, value_sum[:, :HALF], value_sum[:, HALF:])
    own_ref[...] = jnp.concatenate([own_key, own_value], axis=1).astype(BF16)
    tokens.wait(2)
    weights.finish()
    tokens.finish()


def back(
    xg, gq_ref, own_ref, wq_ref, wk_ref, wv_ref,
    gr_ref, kw_ref, vw_ref, qw_ref,
    grads, xc, wkv, term, s1, k1, r1, s2, k2, r2, s3, k3, r3, done_out, done_in,
    d_s, d_r, f_s, f_r, e1_s, e1_r, e2_s, e2_r, e3_s, e3_r,
):
    d = lax.axis_index("dp")
    t = lax.axis_index("tensor")
    barrier = pltpu.get_barrier_semaphore()

    def greet_dp(k, carry):
        pl.semaphore_signal(barrier, inc=1, device_id=(lax.rem(d + k, N_DP), t), device_id_type=MESH)
        return carry

    lax.fori_loop(1, N_DP, greet_dp, 0)
    for link in (1, 2, 6):
        pl.semaphore_signal(barrier, inc=1, device_id=(d, xor_t(t, link)), device_id_type=MESH)
    grads[0:TOK, 0:COLS] = gq_ref[...]
    grads[0:TOK, COLS:WIDE] = own_ref[...]
    wkv[0:HALF] = wk_ref[...]
    wkv[HALF:HD] = wv_ref[...]
    pl.semaphore_wait(barrier, N_DP - 1 + 3)

    place = {}
    for s, mask in enumerate(SLOTS):
        place[mask], place[mask ^ 1] = 2 * s, 2 * s + 1

    def block_of(mask):
        return grads.at[pl.ds(place[mask] * TOK, TOK)]

    def grad_copy(mask, link):
        there = mask ^ link
        return remote(
            block_of(mask), block_of(there), d_s.at[place[there]], d_r.at[place[there]], xor_dp(d, link), t
        )

    def grad_arrival(mask):
        n = place[mask]
        return remote(block_of(mask), block_of(mask), d_s.at[n], d_r.at[n], xor_dp(d, 1), t)

    for link in (8, 2, 6, 1):
        grad_copy(0, link).start()
    onward = {8: (2, 6, 1), 2: (6, 1), 6: (1,), 10: (1,), 14: (2, 1), 4: (1,), 12: (1,)}

    def receive(mask):
        grad_arrival(mask).wait_recv()
        for link in onward.get(mask, ()):
            grad_copy(mask, link).start()

    def multiply(s):
        def part(n, carry):
            cols = rows_at(n * 256, 256, 256)
            own = grads[s * 2 * TOK : (s + 1) * 2 * TOK]
            total = dot_nt(own[:, :COLS], wq_ref[rows_at(n * 256, 256, 256)])
            term[:, cols] = total + dot_nn(own[:, COLS:], wkv[:, cols])
            return carry

        lax.fori_loop(0, 4, part, 0)

    def split(s):
        for e in range(2):
            for j in range(N_T):
                start = e * TOK + ROWS * xor_t(t, j)
                piece = fold(term[rows_at(start, ROWS, 8)]).astype(BF16)
                for o, (g1, g2, g3) in enumerate(ORDERS):
                    kept = [0, g3, g2, g2 ^ g3]
                    to, q = (k1, kept.index(j)) if j in kept else (s1, kept.index(j ^ g1))
                    row = q * 32 + e * 16
                    to[s, o, row : row + 16] = piece[o * 16 : o * 16 + 16]

    def hop(s, o, stage):
        src, dst, send, recv = (
            (s1, r1, e1_s, e1_r), (s2, r2, e2_s, e2_r), (s3, r3, e3_s, e3_r)
        )[stage]
        return remote(
            src.at[s, o], dst.at[s, o], send.at[s, o], recv.at[s, o], d, xor_t(t, ORDERS[o][stage])
        )

    def begin(s):
        split(s)
        for o in range(3):
            hop(s, o, 0).start()

    def second(s):
        for o in range(3):
            hop(s, o, 0).wait_recv()
            s2[s, o] = (k1[s, o, 64:].astype(F32) + r1[s, o, 64:].astype(F32)).astype(BF16)
            hop(s, o, 1).start()
            k2[s, o] = (k1[s, o, :64].astype(F32) + r1[s, o, :64].astype(F32)).astype(BF16)

    def third(s):
        for o in range(3):
            hop(s, o, 1).wait_recv()
            s3[s, o] = (k2[s, o, 32:].astype(F32) + r2[s, o, 32:].astype(F32)).astype(BF16)
            hop(s, o, 2).start()
            k3[s, o] = k2[s, o, :32].astype(F32) + r2[s, o, :32].astype(F32)

    def final_copy(n, mask):
        return remote(done_out.at[n], done_in.at[n], f_s.at[n], f_r.at[n], xor_dp(d, mask), t)

    def last(s):
        for o in range(3):
            hop(s, o, 2).wait_recv()
            total = (k3[s, o] + r3[s, o].astype(F32)).astype(BF16)
            for e in range(2):
                to = done_in if 2 * s + e == 0 else done_out
                to[2 * s + e, o * 16 : o * 16 + 16] = total[e * 16 : e * 16 + 16]
        for e in range(2):
            if 2 * s + e:
                final_copy(2 * s + e, SLOTS[s] ^ e).start()

    def reorder(i, carry):
        s, pair = i // 4, lax.rem(i, 4)
        one = xg[rows_at((2 * pair) * (N_DP * ROWS) + s * 2 * ROWS, 2 * ROWS, 16)].astype(F32)
        two = xg[rows_at((2 * pair + 1) * (N_DP * ROWS) + s * 2 * ROWS, 2 * ROWS, 16)].astype(F32)
        at = s * 2 * TOK + pair * 2 * ROWS
        xc[rows_at(at, 2 * ROWS, 16)] = jnp.concatenate([one[:ROWS], two[:ROWS]], axis=0).astype(BF16)
        xc[rows_at(at + TOK, 2 * ROWS, 16)] = jnp.concatenate([one[ROWS:], two[ROWS:]], axis=0).astype(BF16)
        return carry

    def weight_part(n):
        cols = slice(n * 256, (n + 1) * 256)
        qw_ref[cols] = dot_tn(xc[:, cols], grads[:, :COLS])

    steps = len(SLOTS)
    for s, mask in enumerate(SLOTS):
        if s == 1:
            lax.fori_loop(0, 32, reorder, 0)
            receive(8)
            receive(2)
            receive(6)
        if s == 4:
            receive(10)
            receive(14)
        if s >= 6:
            receive(mask)
        receive(mask ^ 1)
        multiply(s)
        begin(s)
        if s >= 1:
            second(s - 1)
        if s >= 2:
            third(s - 2)
        if s >= 3:
            last(s - 3)
    weight_part(0)
    second(steps - 1)
    third(steps - 2)
    last(steps - 3)
    weight_part(1)
    third(steps - 1)
    last(steps - 2)
    weight_part(2)
    last(steps - 1)
    weight_part(3)

    def pair_weights(n, carry):
        cols = rows_at(n * 256, 256, 256)
        total = dot_tn(grads[:, COLS:], xc[:, cols])
        kw_ref[:, cols] = total[:HALF]
        vw_ref[:, cols] = total[HALF:]
        return carry

    lax.fori_loop(0, 4, pair_weights, 0)
    for s, base in enumerate(SLOTS):
        for e in range(2):
            n, mask = 2 * s + e, base ^ e
            if n:
                final_copy(n, mask).wait()
            gr_ref[:, rows_at(xor_dp(d, mask) * FEAT, FEAT, FEAT)] = unfold(done_in[n].astype(F32)).astype(BF16)
            if n:
                grad_arrival(mask).wait_send()
        for o in range(3):
            for stage in range(3):
                hop(s, o, stage).wait_send()


def vmem(*shape, dtype=BF16):
    return pltpu.VMEM(shape, dtype)


def dma(*shape):
    return pltpu.SemaphoreType.DMA(shape)


def shards(x_rows, w_key, w_value, w_query, queries, grad_out, segment_ids):
    freqs = theta_base ** (-(2.0 * np.arange(HALF, dtype=np.float32)) / HD)
    freqs = jnp.asarray(freqs.astype(np.float32).reshape(1, HALF))
    in_vmem = pl.BlockSpec(memory_space=pltpu.VMEM)
    shape = jax.ShapeDtypeStruct
    key_t, value_t = w_key.T, w_value.T
    limit = 60 * 2**20
    gq, own, tokens = pl.pallas_call(
        front,
        out_shape=(shape((TOK, COLS), BF16), shape((TOK, HD), BF16), shape((N_DP * TOK, FEAT), BF16)),
        in_specs=[in_vmem] * 7,
        out_specs=(in_vmem,) * 3,
        scratch_shapes=[
            vmem(N_DP, 48, 512), vmem(N_DP, 48, 512), vmem(1024, FEAT), vmem(N_DP * ROWS, 1024, dtype=F32),
            vmem(N_DP, 48, 512), vmem(N_DP, 48, 512), vmem(4, 48, HD), vmem(N_T, 48, HD),
            vmem(2 * TOK, HD), vmem(2 * TOK, HD),
            vmem(TOK, HALF, dtype=F32), vmem(TOK, HALF, dtype=F32), vmem(TOK, TOK, dtype=F32),
            vmem(TOK, HD, dtype=F32), vmem(TOK, HD, dtype=F32), vmem(TOK, HD), vmem(TOK, HD),
            dma(N_DP), dma(N_DP), dma(3, 7), dma(3, 7), dma(3, 7), dma(3, 7),
            dma(N_DP), dma(N_DP), dma(N_T), dma(N_T), pltpu.SemaphoreType.DMA, pltpu.SemaphoreType.DMA,
        ],
        compiler_params=pltpu.CompilerParams(
            collective_id=0, has_side_effects=True, vmem_limit_bytes=limit
        ),
        name="front",
    )(x_rows, key_t, value_t, queries, grad_out, segment_ids, freqs)
    rows, key_w, value_w, query_w = pl.pallas_call(
        back,
        out_shape=(
            shape((ROWS, N_DP * FEAT), BF16), shape((HALF, FEAT), F32), shape((HALF, FEAT), F32),
            shape((FEAT, COLS), F32),
        ),
        in_specs=[in_vmem] * 6,
        out_specs=(in_vmem,) * 4,
        scratch_shapes=[
            vmem(N_DP * TOK, WIDE), vmem(N_DP * TOK, FEAT), vmem(HD, FEAT), vmem(2 * TOK, FEAT, dtype=F32),
            vmem(8, 3, 128, 512), vmem(8, 3, 128, 512), vmem(8, 3, 128, 512),
            vmem(8, 3, 64, 512), vmem(8, 3, 64, 512), vmem(8, 3, 64, 512),
            vmem(8, 3, 32, 512), vmem(8, 3, 32, 512, dtype=F32), vmem(8, 3, 32, 512),
            vmem(N_DP, 48, 512), vmem(N_DP, 48, 512),
            dma(N_DP), dma(N_DP), dma(N_DP), dma(N_DP),
            dma(8, 3), dma(8, 3), dma(8, 3), dma(8, 3), dma(8, 3), dma(8, 3),
        ],
        compiler_params=pltpu.CompilerParams(
            collective_id=1, has_side_effects=True, vmem_limit_bytes=limit
        ),
        name="back",
    )(tokens, gq, own, w_query, key_t, value_t)
    return (gq, rows, key_w.T, value_w.T, query_w)


def solution(mesh):
    placed = (
        P(("dp", "tensor"), None),
        P("dp", "tensor"),
        P("dp", "tensor"),
        P("dp", "tensor"),
        P("dp", "tensor"),
        P("dp", "tensor"),
        P("dp", None),
    )
    return jax.shard_map(
        shards,
        mesh=mesh,
        in_specs=placed,
        out_specs=(
            P("dp", "tensor"),
            P(("dp", "tensor"), None),
            P("dp", "tensor"),
            P("dp", "tensor"),
            P("dp", "tensor"),
        ),
        check_vma=False,
    )
```

time: 629 us -> 182 us (0.29)
  waiting for transfers between devices: 433 us -> 0 us
  Pallas kernels: 0 us -> 170 us
  blocking collectives: 106 us -> 0 us
  matrix products: 41.9 us -> 0 us
  between operations: 14.6 us -> 0.67 us
  starting transfers between devices: 9.71 us -> 0 us
  local copies, waits for them, and re-layouts: 18.9 us -> 10.9 us
    reduce_scatter x2 -> x0, waiting for transfers between devices: 176 us -> none  [the longest x1 105 us: shards(): lax.psum_scatter(returned.astype(jnp.float32).astype(jnp.bfloat16), 'tens...]
    pallas_call x0 -> x2, Pallas kernels: none -> 170 us  [the longest x1 88.3 us: shards(): pl.pallas_call(front, out_shape=(shape((TOK, COLS), BF16), shape((TOK, HD...]
    all_gather x2 -> x0, waiting for transfers between devices: 165 us -> none  [the longest x1 134 us: shards(): whole_batch = lax.all_gather(x_rows, 'tensor', axis=0, tiled=True)]
    all_to_all x1 -> x0, waiting for transfers between devices: 86.2 us -> none  [shards(): lax.all_to_all(whole_batch, 'dp', split_axis=1, concat_axis=0, tiled=True)]
    all_to_all x1 -> x0, blocking collectives: 75.9 us -> none  [shards(): lax.all_to_all(term.astype(jnp.bfloat16), 'dp', split_axis=0, concat_axis...]
    dot_general x9 -> x0, matrix products: 38.5 us -> none  [the longest x1 12.8 us: shards(): lax.dot_general(columns, all_query, contract_rows, preferred_element_type...]
    all_gather x1 -> x0, blocking collectives: 30 us -> none  [shards(): lax.all_gather(own_grad, 'dp', axis=0, tiled=True)]
    all_to_all x2 -> x0, local copies, waits for them, and re-layouts: 9.82 us -> none  [the longest x1 6.47 us: shards(): lax.all_to_all(whole_batch, 'dp', split_axis=1, concat_axis=0, tiled=True)]
  transfers between devices with their start and end apart: 8 -> 0, of which waited for: 7 -> 0; matrix products, arithmetic and copies ran while one was open for 4% -> 0% of each run, Pallas kernels for 0% -> 0%
where the time goes in v2:
time: 182 us; the launch traced here: 181 us
  Pallas kernels  170 us (93%)
  local copies, waits for them, and re-layouts  10.9 us (6%)
    pallas_call x1, Pallas kernels, shards(): pl.pallas_call(front, out_shape=(shape((TOK, COLS), BF16), shape((TOK, HD...  88.3 us
    pallas_call x1, Pallas kernels, shards(): pl.pallas_call(back, out_shape=(shape((ROWS, N_DP * FEAT), BF16), shape((...  81.4 us
    unnamed x7, local copies, waits for them, and re-layouts  10.9 us

profile of v2, /device:TPU:1, one launch (start us, length us, event | category | flops | bytes accessed | tf_op | source)
XLA Modules:
  0.0 181.4 jit_solution(11367004328705566271)
XLA Ops:
  0.6 88.3 %front.1 = (bf16[192,1024]{1,0:T(8,128)(2,1)}, bf16[192,128]{1,0:T(8,128)(2,1)}, bf16[3072,1024]{1,0:T(8,128)(2,1)}) custom-call(bf16[24,16384]{1,0:T(8,128)(2,1)} %x_ref.1, bf16[64,1024]{1,0:T(8,128)(2,1)} %bitcast.4, bf16[64,1024]{1,0:T(8,128)(2,1)} %bitcast.6, bf16[192,1024]{1,0:T(8,128)(2,1)} %q_ref.1, bf16[192,1024]{1,0:T(8,128)(2,1)} %do_ref.1, ...), custom_call_target="tpu_custom_call" | custom-call | tf_op jit(solution)/shard_map/front/pallas_call | solution.py:477
  89.0 0.0 copy-start
  89.0 81.4 %back.1 = (bf16[24,16384]{1,0:T(8,128)(2,1)}, f32[64,1024]{1,0:T(8,128)}, f32[64,1024]{1,0:T(8,128)}, f32[1024,1024]{1,0:T(8,128)}) custom-call(bf16[3072,1024]{1,0:T(8,128)(2,1)} %get-tuple-element.13.xg, bf16[192,1024]{1,0:T(8,128)(2,1)} %get-tuple-element.24.gq_ref, bf16[192,128]{1,0:T(8,128)(2,1)} %get-tuple-element.14.own_ref, ...), custom_call_target="tpu_custom_call" | custom-call | tf_op jit(solution)/shard_map/back/pallas_call | solution.py:496
  170.4 0.0 copy-done
  170.4 0.7 copy.18
  171.2 2.1 %copy.19 = bf16[24,16384]{1,0:T(8,128)(2,1)} copy(bf16[24,16384]{1,0:T(8,128)(2,1)} %get-tuple-element.25) | data formatting | bytes 1572864
  173.2 1.7 copy.20
  174.9 1.7 copy.21
  176.6 4.8 %copy.22 = f32[1024,1024]{1,0:T(8,128)} copy(f32[1024,1024]{1,0:T(8,128)} %get-tuple-element.28) | data formatting | bytes 8388608
Async XLA Ops:
  89.0 81.5 %copy-start = (bf16[192,1024]{1,0:T(8,128)(2,1)S(1)}, bf16[192,1024]{1,0:T(8,128)(2,1)}, u32[]{:S(2)}) copy-start(bf16[192,1024]{1,0:T(8,128)(2,1)} %get-tuple-element.24.gq_ref) | copy-start | bytes 1179652

commit v3 on v2

--- a/solution.py
+++ b/solution.py
@@ -1,5 +1,3 @@
-import functools
-
 import jax
 import jax.numpy as jnp
 import numpy as np
@@ -23,7 +21,12 @@
 HALF = 64
 WIDE = COLS + HD
 SLOTS = (0, 2, 6, 8, 10, 14, 4, 12)
-ORDERS = ((1, 2, 6), (2, 6, 1), (6, 1, 2))
+REDUCE = (
+    ((2, 6, 1), (6, 2, 1), (1, 2, 6)),
+    ((2, 6, 1), (6, 2, 1), (6, 1, 2)),
+    ((2, 6, 1), (6, 2, 1), (1, 6, 2)),
+    ((2, 6, 1), (6, 2, 1), (2, 1, 6)),
+)
 
 
 def xor_ring(place, mask):
@@ -80,16 +83,16 @@
 
 
 class Gather:
-    def __init__(self, buf, slot_rows, chunks, send, recv, d, t):
-        self.buf, self.slot_rows, self.chunks = buf, slot_rows, chunks
+    def __init__(self, buf, slot_rows, chunks, orders, send, recv, d, t):
+        self.buf, self.slot_rows, self.chunks, self.orders = buf, slot_rows, chunks, orders
         self.send, self.recv, self.d, self.t = send, recv, d, t
 
     def copies(self, stage, arriving):
         out = []
         for c, (offset, size) in enumerate(self.chunks):
-            first, second, third = ORDERS[c]
+            first, second, third = self.orders[c]
             held = ([0], [0, first], [0, first, second, first ^ second])[stage]
-            link = ORDERS[c][stage]
+            link = self.orders[c][stage]
             for j in held:
                 slot = xor_t(self.t, j ^ link if arriving else j)
                 part = self.buf.at[rows_at(slot * self.slot_rows + offset, size, 16)]
@@ -113,12 +116,15 @@
                 copy.wait_send()
 
 
-def front(
-    x_ref, wk_ref, wv_ref, q_ref, do_ref, seg_ref, freq_ref,
-    gq_ref, own_ref, xg,
-    xsend, xa, wg, kvf, kvsend, kvrecv, heads_out, heads_in, part_out, part_in,
+def kernel(
+    x_ref, wk_ref, wv_ref, seg_ref, freq_ref, q_hbm, do_hbm, wq_hbm,
+    gq_hbm, gr_ref, kw_ref, vw_ref, qw_hbm,
+    q_ref, do_ref, wq_ref, qw_ref,
+    xg, xsend, xa, wg, kvf, kvsend, kvrecv, heads_out, heads_in, part_out, part_in,
     cos_ref, sin_ref, mask_ref, keyp, valuep, key_ref, value_ref,
-    x_s, x_r, w_s, w_r, g_s, g_r, kv_s, kv_r, h_s, h_r, p_s, p_r,
+    grads, xc, term, s1, k1, r1, s2, k2, r2, s3, k3, r3, done_out, done_in,
+    l_s, x_s, x_r, w_s, w_r, g_s, g_r, kv_s, kv_r, h_s, h_r, p_s, p_r,
+    d_s, d_r, f_s, f_r, e1_s, e1_r, e2_s, e2_r, e3_s, e3_r,
 ):
     d = lax.axis_index("dp")
     t = lax.axis_index("tensor")
@@ -134,11 +140,17 @@
 
     lax.fori_loop(1, N_DP, greet_dp, 0)
     lax.fori_loop(1, N_T, greet_t, 0)
+    loads = [
+        pltpu.make_async_copy(src, dst, l_s.at[n])
+        for n, (src, dst) in enumerate(((q_hbm, q_ref), (do_hbm, do_ref), (wq_hbm, wq_ref)))
+    ]
+    for load in loads:
+        load.start()
     wg[rows_at(t * HD, HALF, HALF)] = wk_ref[...]
     wg[rows_at(t * HD + HALF, HALF, HALF)] = wv_ref[...]
     pl.semaphore_wait(barrier, N_DP + N_T - 2)
 
-    weights = Gather(wg, HD, ((0, 48), (48, 48), (96, 32)), w_s, w_r, d, t)
+    weights = Gather(wg, HD, ((0, 64), (64, 64)), ((1, 2, 6), (1, 6, 2)), w_s, w_r, d, t)
     weights.start(0)
 
     def x_copy(k, to):
@@ -181,7 +193,9 @@
     for s, mask in enumerate(SLOTS):
         pair = [unfold(xa[xor_dp(d, mask ^ e)].astype(F32)) for e in range(2)]
         xg[rows_at(t * (N_DP * ROWS) + s * 2 * ROWS, 2 * ROWS, 16)] = jnp.concatenate(pair, axis=0).astype(BF16)
-    tokens = Gather(xg, N_DP * ROWS, ((0, 128), (128, 128), (256, 128)), g_s, g_r, d, t)
+    tokens = Gather(
+        xg, N_DP * ROWS, ((0, 160), (160, 80), (240, 144)), ((1, 2, 6), (2, 6, 1), (6, 1, 2)), g_s, g_r, d, t
+    )
     tokens.start(0)
 
     weights.wait(2)
@@ -193,8 +207,8 @@
 
     lax.fori_loop(0, 4, project, 0)
 
-    def kv_copy(mask, to, slot):
-        return remote(kvsend.at[mask], kvrecv.at[slot], kv_s.at[mask], kv_r.at[mask], to, t)
+    def kv_copy(mask):
+        return remote(kvsend.at[mask], kvrecv.at[mask], kv_s.at[mask], kv_r.at[mask], xor_dp(d, mask), t)
 
     for s, base in enumerate(SLOTS):
         for e in range(2):
@@ -204,11 +218,11 @@
                 kvrecv[0] = block
             else:
                 kvsend[mask] = block
-                kv_copy(mask, xor_dp(d, mask), mask).start()
+                kv_copy(mask).start()
     tokens.wait(0)
     tokens.start(1)
     for mask in range(1, N_DP):
-        kv_copy(mask, xor_dp(d, mask), mask).wait()
+        kv_copy(mask).wait()
 
     def add_kv(k, total):
         return total + kvrecv[k].astype(F32)
@@ -227,8 +241,6 @@
 
     lax.fori_loop(1, N_T, send_heads, 0)
     heads_in[t] = heads_out[t // 2]
-    tokens.wait(1)
-    tokens.start(2)
 
     def wait_heads(k, carry):
         head_copy(k, lax.rem(t + k, N_T)).wait_send()
@@ -237,16 +249,20 @@
         return carry
 
     lax.fori_loop(1, N_T, wait_heads, 0)
+    tokens.wait(1)
+    tokens.start(2)
     blocks = [heads_in[i].astype(F32) for i in range(N_T)]
     first = jnp.concatenate([b[:ROWS] for b in blocks], axis=0)
-    second = jnp.concatenate([b[ROWS:] for b in blocks], axis=0)
+    second_part = jnp.concatenate([b[ROWS:] for b in blocks], axis=0)
     cosine, sine = cos_ref[...], sin_ref[...]
-    a, c = first[:, :HALF], second[:, :HALF]
+    a, c = first[:, :HALF], second_part[:, :HALF]
     key_ref[...] = jnp.concatenate([a * cosine - c * sine, c * cosine + a * sine], axis=1).astype(BF16)
-    value_ref[...] = jnp.concatenate([first[:, HALF:], second[:, HALF:]], axis=1).astype(BF16)
+    value_ref[...] = jnp.concatenate([first[:, HALF:], second_part[:, HALF:]], axis=1).astype(BF16)
     keyp[...] = jnp.zeros_like(keyp)
     valuep[...] = jnp.zeros_like(valuep)
     scale = 1.0 / HD**0.5
+    for load in loads:
+        load.wait()
 
     def head_step(h, carry):
         cols = rows_at(h * HD, HD, HD)
@@ -258,7 +274,7 @@
         dprob = dot_nt(do, value)
         delta = jnp.sum(probs * dprob, axis=1, keepdims=True)
         dscore = (probs * (dprob - delta)).astype(BF16)
-        gq_ref[:, cols] = (dot_nn(dscore, key) * scale).astype(BF16)
+        grads[0:TOK, cols] = (dot_nn(dscore, key) * scale).astype(BF16)
         keyp[...] += dot_tn(dscore, q)
         valuep[...] += dot_tn(probs.astype(BF16), do)
         return carry
@@ -276,34 +292,7 @@
     is_first = lax.rem(t, 2) == 0
     own_key = jnp.where(is_first, upper * cosine + lower * sine, lower * cosine - upper * sine)
     own_value = jnp.where(is_first, value_sum[:, :HALF], value_sum[:, HALF:])
-    own_ref[...] = jnp.concatenate([own_key, own_value], axis=1).astype(BF16)
-    tokens.wait(2)
-    weights.finish()
-    tokens.finish()
-
-
-def back(
-    xg, gq_ref, own_ref, wq_ref, wk_ref, wv_ref,
-    gr_ref, kw_ref, vw_ref, qw_ref,
-    grads, xc, wkv, term, s1, k1, r1, s2, k2, r2, s3, k3, r3, done_out, done_in,
-    d_s, d_r, f_s, f_r, e1_s, e1_r, e2_s, e2_r, e3_s, e3_r,
-):
-    d = lax.axis_index("dp")
-    t = lax.axis_index("tensor")
-    barrier = pltpu.get_barrier_semaphore()
-
-    def greet_dp(k, carry):
-        pl.semaphore_signal(barrier, inc=1, device_id=(lax.rem(d + k, N_DP), t), device_id_type=MESH)
-        return carry
-
-    lax.fori_loop(1, N_DP, greet_dp, 0)
-    for link in (1, 2, 6):
-        pl.semaphore_signal(barrier, inc=1, device_id=(d, xor_t(t, link)), device_id_type=MESH)
-    grads[0:TOK, 0:COLS] = gq_ref[...]
-    grads[0:TOK, COLS:WIDE] = own_ref[...]
-    wkv[0:HALF] = wk_ref[...]
-    wkv[HALF:HD] = wv_ref[...]
-    pl.semaphore_wait(barrier, N_DP - 1 + 3)
+    grads[0:TOK, COLS:WIDE] = jnp.concatenate([own_key, own_value], axis=1).astype(BF16)
 
     place = {}
     for s, mask in enumerate(SLOTS):
@@ -324,19 +313,22 @@
 
     for link in (8, 2, 6, 1):
         grad_copy(0, link).start()
+    gq_out = pltpu.make_async_copy(grads.at[0:TOK, 0:COLS], gq_hbm, l_s.at[3])
+    gq_out.start()
     onward = {8: (2, 6, 1), 2: (6, 1), 6: (1,), 10: (1,), 14: (2, 1), 4: (1,), 12: (1,)}
 
-    def receive(mask):
-        grad_arrival(mask).wait_recv()
-        for link in onward.get(mask, ()):
-            grad_copy(mask, link).start()
+    def receive(*masks):
+        for mask in masks:
+            grad_arrival(mask).wait_recv()
+            for link in onward.get(mask, ()):
+                grad_copy(mask, link).start()
 
     def multiply(s):
         def part(n, carry):
             cols = rows_at(n * 256, 256, 256)
             own = grads[s * 2 * TOK : (s + 1) * 2 * TOK]
             total = dot_nt(own[:, :COLS], wq_ref[rows_at(n * 256, 256, 256)])
-            term[:, cols] = total + dot_nn(own[:, COLS:], wkv[:, cols])
+            term[:, cols] = total + dot_nn(own[:, COLS:], wg[rows_at(t * HD, HD, HD), cols])
             return carry
 
         lax.fori_loop(0, 4, part, 0)
@@ -346,7 +338,7 @@
             for j in range(N_T):
                 start = e * TOK + ROWS * xor_t(t, j)
                 piece = fold(term[rows_at(start, ROWS, 8)]).astype(BF16)
-                for o, (g1, g2, g3) in enumerate(ORDERS):
+                for o, (g1, g2, g3) in enumerate(REDUCE[s % 4]):
                     kept = [0, g3, g2, g2 ^ g3]
                     to, q = (k1, kept.index(j)) if j in kept else (s1, kept.index(j ^ g1))
                     row = q * 32 + e * 16
@@ -357,10 +349,11 @@
             (s1, r1, e1_s, e1_r), (s2, r2, e2_s, e2_r), (s3, r3, e3_s, e3_r)
         )[stage]
         return remote(
-            src.at[s, o], dst.at[s, o], send.at[s, o], recv.at[s, o], d, xor_t(t, ORDERS[o][stage])
+            src.at[s, o], dst.at[s, o], send.at[s, o], recv.at[s, o], d, xor_t(t, REDUCE[s % 4][o][stage])
         )
 
     def begin(s):
+        multiply(s)
         split(s)
         for o in range(3):
             hop(s, o, 0).start()
@@ -402,41 +395,14 @@
         xc[rows_at(at + TOK, 2 * ROWS, 16)] = jnp.concatenate([one[ROWS:], two[ROWS:]], axis=0).astype(BF16)
         return carry
 
+    def weight_copy(n):
+        rows = pl.ds(n * 256, 256)
+        return pltpu.make_async_copy(qw_ref.at[rows], qw_hbm.at[rows], l_s.at[4 + n])
+
     def weight_part(n):
         cols = slice(n * 256, (n + 1) * 256)
         qw_ref[cols] = dot_tn(xc[:, cols], grads[:, :COLS])
-
-    steps = len(SLOTS)
-    for s, mask in enumerate(SLOTS):
-        if s == 1:
-            lax.fori_loop(0, 32, reorder, 0)
-            receive(8)
-            receive(2)
-            receive(6)
-        if s == 4:
-            receive(10)
-            receive(14)
-        if s >= 6:
-            receive(mask)
-        receive(mask ^ 1)
-        multiply(s)
-        begin(s)
-        if s >= 1:
-            second(s - 1)
-        if s >= 2:
-            third(s - 2)
-        if s >= 3:
-            last(s - 3)
-    weight_part(0)
-    second(steps - 1)
-    third(steps - 2)
-    last(steps - 3)
-    weight_part(1)
-    third(steps - 1)
-    last(steps - 2)
-    weight_part(2)
-    last(steps - 1)
-    weight_part(3)
+        weight_copy(n).start()
 
     def pair_weights(n, carry):
         cols = rows_at(n * 256, 256, 256)
@@ -445,6 +411,54 @@
         vw_ref[:, cols] = total[HALF:]
         return carry
 
+    receive(1)
+    begin(0)
+    receive(8, 2, 6)
+    second(0)
+    receive(3)
+    begin(1)
+    third(0)
+    receive(7)
+    begin(2)
+    second(1)
+    receive(9)
+    begin(3)
+    last(0)
+    second(2)
+    third(1)
+    receive(10, 14)
+    second(3)
+    receive(11)
+    begin(4)
+    third(2)
+    last(1)
+    receive(15)
+    begin(5)
+    tokens.wait(2)
+    lax.fori_loop(0, 32, reorder, 0)
+    second(4)
+    third(3)
+    last(2)
+    receive(4, 12, 5)
+    begin(6)
+    second(5)
+    third(4)
+    last(3)
+    receive(13)
+    begin(7)
+    weight_part(0)
+    second(6)
+    third(5)
+    last(4)
+    weight_part(1)
+    second(7)
+    third(6)
+    last(5)
+    weight_part(2)
+    third(7)
+    last(6)
+    weight_part(3)
+    last(7)
     lax.fori_loop(0, 4, pair_weights, 0)
     for s, base in enumerate(SLOTS):
         for e in range(2):
@@ -457,6 +471,27 @@
         for o in range(3):
             for stage in range(3):
                 hop(s, o, stage).wait_send()
+    weights.finish()
+    tokens.finish()
+    gq_out.wait()
+    for n in range(4):
+        weight_copy(n).wait()
+
+
+def emit(*refs):
+    count = len(refs) // 2
+    sems = refs[-1]
+    copies = []
+    for src, dst in zip(refs[:count], refs[count : 2 * count]):
+        parts = 4 if src.shape[0] >= FEAT else 1
+        size = src.shape[0] // parts
+        for n in range(parts):
+            rows = pl.ds(n * size, size)
+            copies.append(pltpu.make_async_copy(src.at[rows], dst.at[rows], sems.at[len(copies)]))
+    for copy in copies:
+        copy.start()
+    for copy in copies:
+        copy.wait()
 
 
 def vmem(*shape, dtype=BF16):
@@ -471,50 +506,47 @@
     freqs = theta_base ** (-(2.0 * np.arange(HALF, dtype=np.float32)) / HD)
     freqs = jnp.asarray(freqs.astype(np.float32).reshape(1, HALF))
     in_vmem = pl.BlockSpec(memory_space=pltpu.VMEM)
+    anywhere = pl.BlockSpec(memory_space=pl.ANY)
     shape = jax.ShapeDtypeStruct
-    key_t, value_t = w_key.T, w_value.T
-    limit = 60 * 2**20
-    gq, own, tokens = pl.pallas_call(
-        front,
-        out_shape=(shape((TOK, COLS), BF16), shape((TOK, HD), BF16), shape((N_DP * TOK, FEAT), BF16)),
-        in_specs=[in_vmem] * 7,
-        out_specs=(in_vmem,) * 3,
+    results = (
+        shape((TOK, COLS), BF16), shape((ROWS, N_DP * FEAT), BF16), shape((HALF, FEAT), F32),
+        shape((HALF, FEAT), F32), shape((FEAT, COLS), F32),
+    )
+    outs = pl.pallas_call(
+        kernel,
+        out_shape=results,
+        in_specs=[in_vmem] * 5 + [anywhere] * 3,
+        out_specs=(anywhere, in_vmem, in_vmem, in_vmem, anywhere),
         scratch_shapes=[
-            vmem(N_DP, 48, 512), vmem(N_DP, 48, 512), vmem(1024, FEAT), vmem(N_DP * ROWS, 1024, dtype=F32),
-            vmem(N_DP, 48, 512), vmem(N_DP, 48, 512), vmem(4, 48, HD), vmem(N_T, 48, HD),
-            vmem(2 * TOK, HD), vmem(2 * TOK, HD),
+            vmem(TOK, COLS), vmem(TOK, COLS), vmem(FEAT, COLS), vmem(FEAT, COLS, dtype=F32),
+            vmem(N_DP * TOK, FEAT), vmem(N_DP, 48, 512), vmem(N_DP, 48, 512), vmem(1024, FEAT),
+            vmem(N_DP * ROWS, 1024, dtype=F32), vmem(N_DP, 48, 512), vmem(N_DP, 48, 512),
+            vmem(4, 48, HD), vmem(N_T, 48, HD), vmem(2 * TOK, HD), vmem(2 * TOK, HD),
             vmem(TOK, HALF, dtype=F32), vmem(TOK, HALF, dtype=F32), vmem(TOK, TOK, dtype=F32),
             vmem(TOK, HD, dtype=F32), vmem(TOK, HD, dtype=F32), vmem(TOK, HD), vmem(TOK, HD),
-            dma(N_DP), dma(N_DP), dma(3, 7), dma(3, 7), dma(3, 7), dma(3, 7),
-            dma(N_DP), dma(N_DP), dma(N_T), dma(N_T), pltpu.SemaphoreType.DMA, pltpu.SemaphoreType.DMA,
-        ],
-        compiler_params=pltpu.CompilerParams(
-            collective_id=0, has_side_effects=True, vmem_limit_bytes=limit
-        ),
-        name="front",
-    )(x_rows, key_t, value_t, queries, grad_out, segment_ids, freqs)
-    rows, key_w, value_w, query_w = pl.pallas_call(
-        back,
-        out_shape=(
-            shape((ROWS, N_DP * FEAT), BF16), shape((HALF, FEAT), F32), shape((HALF, FEAT), F32),
-            shape((FEAT, COLS), F32),
-        ),
-        in_specs=[in_vmem] * 6,
-        out_specs=(in_vmem,) * 4,
-        scratch_shapes=[
-            vmem(N_DP * TOK, WIDE), vmem(N_DP * TOK, FEAT), vmem(HD, FEAT), vmem(2 * TOK, FEAT, dtype=F32),
+            vmem(N_DP * TOK, WIDE), vmem(N_DP * TOK, FEAT), vmem(2 * TOK, FEAT, dtype=F32),
             vmem(8, 3, 128, 512), vmem(8, 3, 128, 512), vmem(8, 3, 128, 512),
             vmem(8, 3, 64, 512), vmem(8, 3, 64, 512), vmem(8, 3, 64, 512),
             vmem(8, 3, 32, 512), vmem(8, 3, 32, 512, dtype=F32), vmem(8, 3, 32, 512),
             vmem(N_DP, 48, 512), vmem(N_DP, 48, 512),
+            dma(8), dma(N_DP), dma(N_DP), dma(2, 7), dma(2, 7), dma(3, 7), dma(3, 7),
+            dma(N_DP), dma(N_DP), dma(N_T), dma(N_T), pltpu.SemaphoreType.DMA, pltpu.SemaphoreType.DMA,
             dma(N_DP), dma(N_DP), dma(N_DP), dma(N_DP),
             dma(8, 3), dma(8, 3), dma(8, 3), dma(8, 3), dma(8, 3), dma(8, 3),
         ],
         compiler_params=pltpu.CompilerParams(
-            collective_id=1, has_side_effects=True, vmem_limit_bytes=limit
+            collective_id=0, has_side_effects=True, vmem_limit_bytes=62 * 2**20
         ),
-        name="back",
-    )(tokens, gq, own, w_query, key_t, value_t)
+        name="grads",
+    )(x_rows, w_key.T, w_value.T, segment_ids, freqs, queries, grad_out, w_query)
+    gq, rows, key_w, value_w, query_w = pl.pallas_call(
+        emit,
+        out_shape=results,
+        in_specs=[anywhere] * 5,
+        out_specs=(anywhere,) * 5,
+        scratch_shapes=[dma(8)],
+        name="emit",
+    )(*outs)
     return (gq, rows, key_w.T, value_w.T, query_w)
 
 

time: 182 us -> 333 us (1.83)
  Pallas kernels: 170 us -> 333 us
  local copies, waits for them, and re-layouts: 10.9 us -> 0 us
    pallas_call x2, Pallas kernels: 170 us -> 333 us  [the longest x1 180 us: shards(): pl.pallas_call(emit, out_shape=results, in_specs=[anywhere] * 5, out_spec...]
    unnamed x7 -> x0, local copies, waits for them, and re-layouts: 10.9 us -> none
where the time goes in v3:
time: 333 us
  Pallas kernels  333 us (100%)
    pallas_call x1, Pallas kernels, shards(): pl.pallas_call(emit, out_shape=results, in_specs=[anywhere] * 5, out_spec...  180 us
    pallas_call x1, Pallas kernels, shards(): pl.pallas_call(kernel, out_shape=results, in_specs=[in_vmem] * 5 + [anywh...  153 us

profile of v3, /device:TPU:1, one launch (start us, length us, event | category | flops | bytes accessed | tf_op | source)
XLA Modules:
  0.0 333.3 jit_solution(8159337717393025069)
XLA Ops:
  0.6 152.9 %grads.1 = (bf16[192,1024]{1,0:T(8,128)(2,1)}, bf16[24,16384]{1,0:T(8,128)(2,1)}, f32[64,1024]{1,0:T(8,128)}, f32[64,1024]{1,0:T(8,128)}, f32[1024,1024]{1,0:T(8,128)}) custom-call(bf16[24,16384]{1,0:T(8,128)(2,1)} %x_ref.1, bf16[64,1024]{1,0:T(8,128)(2,1)} %bitcast.4, bf16[64,1024]{1,0:T(8,128)(2,1)} %bitcast.5, s32[1,192]{1,0:T(1,128)} %seg_ref.1, ...), custom_call_target="tpu_custom_call" | custom-call | tf_op jit(solution)/shard_map/grads/pallas_call | solution.py:515
  153.5 179.8 %emit.1 = (bf16[192,1024]{1,0:T(8,128)(2,1)}, bf16[24,16384]{1,0:T(8,128)(2,1)}, f32[64,1024]{1,0:T(8,128)}, f32[64,1024]{1,0:T(8,128)}, f32[1024,1024]{1,0:T(8,128)}) custom-call(bf16[192,1024]{1,0:T(8,128)(2,1)} %get-tuple-element.15.refs_0_, bf16[24,16384]{1,0:T(8,128)(2,1)} %get-tuple-element.16.refs_1_, f32[64,1024]{1,0:T(8,128)} %get-tuple-element.17.refs_2_, ...), custom_call_target="tpu_custom_call" | custom-call | tf_op jit(solution)/shard_map/emit/pallas_call | solution.py:542

commit v4 on v3

--- a/solution.py
+++ b/solution.py
@@ -21,12 +21,7 @@
 HALF = 64
 WIDE = COLS + HD
 SLOTS = (0, 2, 6, 8, 10, 14, 4, 12)
-REDUCE = (
-    ((2, 6, 1), (6, 2, 1), (1, 2, 6)),
-    ((2, 6, 1), (6, 2, 1), (6, 1, 2)),
-    ((2, 6, 1), (6, 2, 1), (1, 6, 2)),
-    ((2, 6, 1), (6, 2, 1), (2, 1, 6)),
-)
+ORDERS = ((1, 2, 6), (2, 6, 1), (6, 1, 2))
 
 
 def xor_ring(place, mask):
@@ -87,9 +82,10 @@
         self.buf, self.slot_rows, self.chunks, self.orders = buf, slot_rows, chunks, orders
         self.send, self.recv, self.d, self.t = send, recv, d, t
 
-    def copies(self, stage, arriving):
+    def copies(self, stage, arriving, only=(1, 2, 0)):
         out = []
-        for c, (offset, size) in enumerate(self.chunks):
+        for c in only:
+            offset, size = self.chunks[c]
             first, second, third = self.orders[c]
             held = ([0], [0, first], [0, first, second, first ^ second])[stage]
             link = self.orders[c][stage]
@@ -110,6 +106,13 @@
         for copy in self.copies(stage, True):
             copy.wait_recv()
 
+    def step(self, stage):
+        for c in (1, 2, 0):
+            for copy in self.copies(stage, True, (c,)):
+                copy.wait_recv()
+            for copy in self.copies(stage + 1, False, (c,)):
+                copy.start()
+
     def finish(self):
         for stage in range(3):
             for copy in self.copies(stage, False):
@@ -120,7 +123,7 @@
     x_ref, wk_ref, wv_ref, seg_ref, freq_ref, q_hbm, do_hbm, wq_hbm,
     gq_hbm, gr_ref, kw_ref, vw_ref, qw_hbm,
     q_ref, do_ref, wq_ref, qw_ref,
-    xg, xsend, xa, wg, kvf, kvsend, kvrecv, heads_out, heads_in, part_out, part_in,
+    xg, xa, wg, kvf, kvsend, kvswap, kvrecv, heads_out, heads_in, part_out, part_in,
     cos_ref, sin_ref, mask_ref, keyp, valuep, key_ref, value_ref,
     grads, xc, term, s1, k1, r1, s2, k2, r2, s3, k3, r3, done_out, done_in,
     l_s, x_s, x_r, w_s, w_r, g_s, g_r, kv_s, kv_r, h_s, h_r, p_s, p_r,
@@ -150,23 +153,23 @@
     wg[rows_at(t * HD + HALF, HALF, HALF)] = wv_ref[...]
     pl.semaphore_wait(barrier, N_DP + N_T - 2)
 
-    weights = Gather(wg, HD, ((0, 64), (64, 64)), ((1, 2, 6), (1, 6, 2)), w_s, w_r, d, t)
+    weights = Gather(wg, HD, ((0, 48), (48, 32), (80, 48)), ORDERS, w_s, w_r, d, t)
     weights.start(0)
 
-    def x_copy(k, to):
-        return remote(xsend.at[to], xa.at[d], x_s.at[k], x_r.at[k], to, t)
-
-    def pack_x(k, carry):
+    def x_copy(k):
         to = lax.rem(d + k, N_DP)
-        block = x_ref[:, rows_at(to * FEAT, FEAT, FEAT)].astype(F32)
-        xsend[to] = fold(block).astype(BF16)
-        x_copy(k, to).start()
-        return carry
-
-    lax.fori_loop(1, N_DP, pack_x, 0)
-    xa[d] = fold(x_ref[:, rows_at(d * FEAT, FEAT, FEAT)].astype(F32)).astype(BF16)
-    weights.wait(0)
-    weights.start(1)
+        return remote(
+            x_ref.at[:, rows_at(to * FEAT, FEAT, FEAT)], xa.at[d], x_s.at[k], x_r.at[k], to, t
+        )
+
+    def send_x(k, carry):
+        x_copy(k).start()
+        return carry
+
+    lax.fori_loop(1, N_DP, send_x, 0)
+    weights.step(0)
+    weights.step(1)
+    xa[d] = x_ref[:, rows_at(d * FEAT, FEAT, FEAT)]
 
     row_no = lax.broadcasted_iota(jnp.int32, (TOK, TOK), 0)
     col_no = lax.broadcasted_iota(jnp.int32, (TOK, TOK), 1)
@@ -179,22 +182,18 @@
     sin_ref[...] = jnp.sin(angle)
     mask_ref[...] = ((seg_row == seg_col) & (col_no <= row_no)).astype(F32)
 
-    weights.wait(1)
-    weights.start(2)
-
     def wait_x(k, carry):
-        x_copy(k, lax.rem(d + k, N_DP)).wait_send()
-        remote(
-            xsend.at[d], xa.at[lax.rem(d + N_DP - k, N_DP)], x_s.at[k], x_r.at[k], d, t
-        ).wait_recv()
+        x_copy(k).wait_send()
+        slot = xa.at[lax.rem(d + N_DP - k, N_DP)]
+        remote(slot, slot, x_s.at[k], x_r.at[k], d, t).wait_recv()
         return carry
 
     lax.fori_loop(1, N_DP, wait_x, 0)
     for s, mask in enumerate(SLOTS):
-        pair = [unfold(xa[xor_dp(d, mask ^ e)].astype(F32)) for e in range(2)]
+        pair = [xa[xor_dp(d, mask ^ e)].astype(F32) for e in range(2)]
         xg[rows_at(t * (N_DP * ROWS) + s * 2 * ROWS, 2 * ROWS, 16)] = jnp.concatenate(pair, axis=0).astype(BF16)
     tokens = Gather(
-        xg, N_DP * ROWS, ((0, 160), (160, 80), (240, 144)), ((1, 2, 6), (2, 6, 1), (6, 1, 2)), g_s, g_r, d, t
+        xg, N_DP * ROWS, ((0, 160), (160, 80), (240, 144)), ORDERS, g_s, g_r, d, t
     )
     tokens.start(0)
 
@@ -207,27 +206,28 @@
 
     lax.fori_loop(0, 4, project, 0)
 
-    def kv_copy(mask):
-        return remote(kvsend.at[mask], kvrecv.at[mask], kv_s.at[mask], kv_r.at[mask], xor_dp(d, mask), t)
-
-    for s, base in enumerate(SLOTS):
-        for e in range(2):
-            mask = base ^ e
-            block = fold(kvf[(2 * s + e) * ROWS : (2 * s + e + 1) * ROWS]).astype(BF16)
-            if mask == 0:
-                kvrecv[0] = block
-            else:
-                kvsend[mask] = block
-                kv_copy(mask).start()
-    tokens.wait(0)
-    tokens.start(1)
-    for mask in range(1, N_DP):
-        kv_copy(mask).wait()
-
-    def add_kv(k, total):
-        return total + kvrecv[k].astype(F32)
-
-    lin = lax.fori_loop(1, N_DP, add_kv, kvrecv[0].astype(F32))
+    swap = remote(kvsend.at[1], kvswap, kv_s.at[0], kv_r.at[0], xor_dp(d, 1), t)
+
+    def kv_copy(s):
+        return remote(
+            kvsend.at[0, s], kvrecv.at[s], kv_s.at[s], kv_r.at[s], xor_dp(d, SLOTS[s]), t
+        )
+
+    def kv_part(n):
+        return fold(kvf[n * ROWS : (n + 1) * ROWS])
+
+    for s in range(len(SLOTS)):
+        kvsend[1, s] = kv_part(2 * s + 1).astype(BF16)
+    swap.start()
+    swap.wait()
+    for s in range(1, len(SLOTS)):
+        kvsend[0, s] = (kv_part(2 * s) + kvswap[s].astype(F32)).astype(BF16)
+        kv_copy(s).start()
+    tokens.step(0)
+    lin = kv_part(0) + kvswap[0].astype(F32)
+    for s in range(1, len(SLOTS)):
+        kv_copy(s).wait()
+        lin = lin + kvrecv[s].astype(F32)
     for head in range(4):
         rows = lin[(head // 2) * ROWS : (head // 2 + 1) * ROWS, (head % 2) * 256 : (head % 2 + 1) * 256]
         heads_out[head] = jnp.concatenate([rows[:, :HD], rows[:, HD:]], axis=0).astype(BF16)
@@ -249,8 +249,7 @@
         return carry
 
     lax.fori_loop(1, N_T, wait_heads, 0)
-    tokens.wait(1)
-    tokens.start(2)
+    tokens.step(1)
     blocks = [heads_in[i].astype(F32) for i in range(N_T)]
     first = jnp.concatenate([b[:ROWS] for b in blocks], axis=0)
     second_part = jnp.concatenate([b[ROWS:] for b in blocks], axis=0)
@@ -315,13 +314,15 @@
         grad_copy(0, link).start()
     gq_out = pltpu.make_async_copy(grads.at[0:TOK, 0:COLS], gq_hbm, l_s.at[3])
     gq_out.start()
-    onward = {8: (2, 6, 1), 2: (6, 1), 6: (1,), 10: (1,), 14: (2, 1), 4: (1,), 12: (1,)}
+    onward = {8: (2, 6, 1), 2: (1,), 6: (1,), 10: (1,), 14: (2, 1), 4: (1,), 12: (1,)}
 
     def receive(*masks):
         for mask in masks:
             grad_arrival(mask).wait_recv()
             for link in onward.get(mask, ()):
                 grad_copy(mask, link).start()
+            if mask == 14:
+                grad_copy(2, 6).start()
 
     def multiply(s):
         def part(n, carry):
@@ -338,7 +339,7 @@
             for j in range(N_T):
                 start = e * TOK + ROWS * xor_t(t, j)
                 piece = fold(term[rows_at(start, ROWS, 8)]).astype(BF16)
-                for o, (g1, g2, g3) in enumerate(REDUCE[s % 4]):
+                for o, (g1, g2, g3) in enumerate(ORDERS):
                     kept = [0, g3, g2, g2 ^ g3]
                     to, q = (k1, kept.index(j)) if j in kept else (s1, kept.index(j ^ g1))
                     row = q * 32 + e * 16
@@ -349,7 +350,7 @@
             (s1, r1, e1_s, e1_r), (s2, r2, e2_s, e2_r), (s3, r3, e3_s, e3_r)
         )[stage]
         return remote(
-            src.at[s, o], dst.at[s, o], send.at[s, o], recv.at[s, o], d, xor_t(t, REDUCE[s % 4][o][stage])
+            src.at[s, o], dst.at[s, o], send.at[s, o], recv.at[s, o], d, xor_t(t, ORDERS[o][stage])
         )
 
     def begin(s):
@@ -399,10 +400,17 @@
         rows = pl.ds(n * 256, 256)
         return pltpu.make_async_copy(qw_ref.at[rows], qw_hbm.at[rows], l_s.at[4 + n])
 
-    def weight_part(n):
+    deep = 8 * TOK
+
+    def weight_part(n, part):
         cols = slice(n * 256, (n + 1) * 256)
-        qw_ref[cols] = dot_tn(xc[:, cols], grads[:, :COLS])
-        weight_copy(n).start()
+        rows = slice(part * deep, (part + 1) * deep)
+        total = dot_tn(xc[rows, cols], grads[rows, :COLS])
+        if part == 0:
+            qw_ref[cols] = total
+        else:
+            qw_ref[cols] += total
+            weight_copy(n).start()
 
     def pair_weights(n, carry):
         cols = rows_at(n * 256, 256, 256)
@@ -417,48 +425,53 @@
     second(0)
     receive(3)
     begin(1)
-    third(0)
     receive(7)
     begin(2)
-    second(1)
     receive(9)
     begin(3)
-    last(0)
-    second(2)
-    third(1)
     receive(10, 14)
-    second(3)
+    third(0)
+    second(1)
     receive(11)
     begin(4)
+    second(2)
+    receive(15)
+    begin(5)
+    third(1)
+    last(0)
+    second(3)
+    tokens.wait(2)
+    lax.fori_loop(0, 32, reorder, 0)
     third(2)
     last(1)
-    receive(15)
-    begin(5)
-    tokens.wait(2)
-    lax.fori_loop(0, 32, reorder, 0)
     second(4)
+    receive(4, 12)
     third(3)
     last(2)
-    receive(4, 12, 5)
+    second(5)
+    receive(5)
     begin(6)
-    second(5)
+    receive(13)
+    begin(7)
     third(4)
     last(3)
-    receive(13)
-    begin(7)
-    weight_part(0)
-    second(6)
+    weight_part(0, 0)
     third(5)
     last(4)
-    weight_part(1)
+    second(6)
+    weight_part(0, 1)
     second(7)
+    last(5)
+    weight_part(1, 0)
     third(6)
-    last(5)
-    weight_part(2)
+    weight_part(1, 1)
     third(7)
     last(6)
-    weight_part(3)
+    weight_part(2, 0)
+    weight_part(2, 1)
     last(7)
+    weight_part(3, 0)
+    weight_part(3, 1)
     lax.fori_loop(0, 4, pair_weights, 0)
     for s, base in enumerate(SLOTS):
         for e in range(2):
@@ -479,19 +492,23 @@
 
 
 def emit(*refs):
-    count = len(refs) // 2
-    sems = refs[-1]
-    copies = []
-    for src, dst in zip(refs[:count], refs[count : 2 * count]):
+    count = len(refs) // 3
+    sources, targets, held, (sem_in, sem_out) = refs[:count], refs[count : 2 * count], refs[2 * count : -2], refs[-2:]
+    loads, stores = [], []
+    for src, dst, mid in zip(sources, targets, held):
         parts = 4 if src.shape[0] >= FEAT else 1
         size = src.shape[0] // parts
         for n in range(parts):
             rows = pl.ds(n * size, size)
-            copies.append(pltpu.make_async_copy(src.at[rows], dst.at[rows], sems.at[len(copies)]))
-    for copy in copies:
-        copy.start()
-    for copy in copies:
-        copy.wait()
+            loads.append(pltpu.make_async_copy(src.at[rows], mid.at[rows], sem_in.at[len(loads)]))
+            stores.append(pltpu.make_async_copy(mid.at[rows], dst.at[rows], sem_out.at[len(stores)]))
+    for load in loads:
+        load.start()
+    for load, store in zip(loads, stores):
+        load.wait()
+        store.start()
+    for store in stores:
+        store.wait()
 
 
 def vmem(*shape, dtype=BF16):
@@ -519,8 +536,8 @@
         out_specs=(anywhere, in_vmem, in_vmem, in_vmem, anywhere),
         scratch_shapes=[
             vmem(TOK, COLS), vmem(TOK, COLS), vmem(FEAT, COLS), vmem(FEAT, COLS, dtype=F32),
-            vmem(N_DP * TOK, FEAT), vmem(N_DP, 48, 512), vmem(N_DP, 48, 512), vmem(1024, FEAT),
-            vmem(N_DP * ROWS, 1024, dtype=F32), vmem(N_DP, 48, 512), vmem(N_DP, 48, 512),
+            vmem(N_DP * TOK, FEAT), vmem(N_DP, ROWS, FEAT), vmem(1024, FEAT),
+            vmem(N_DP * ROWS, 1024, dtype=F32), vmem(2, 8, 48, 512), vmem(8, 48, 512), vmem(8, 48, 512),
             vmem(4, 48, HD), vmem(N_T, 48, HD), vmem(2 * TOK, HD), vmem(2 * TOK, HD),
             vmem(TOK, HALF, dtype=F32), vmem(TOK, HALF, dtype=F32), vmem(TOK, TOK, dtype=F32),
             vmem(TOK, HD, dtype=F32), vmem(TOK, HD, dtype=F32), vmem(TOK, HD), vmem(TOK, HD),
@@ -529,8 +546,8 @@
             vmem(8, 3, 64, 512), vmem(8, 3, 64, 512), vmem(8, 3, 64, 512),
             vmem(8, 3, 32, 512), vmem(8, 3, 32, 512, dtype=F32), vmem(8, 3, 32, 512),
             vmem(N_DP, 48, 512), vmem(N_DP, 48, 512),
-            dma(8), dma(N_DP), dma(N_DP), dma(2, 7), dma(2, 7), dma(3, 7), dma(3, 7),
-            dma(N_DP), dma(N_DP), dma(N_T), dma(N_T), pltpu.SemaphoreType.DMA, pltpu.SemaphoreType.DMA,
+            dma(8), dma(N_DP), dma(N_DP), dma(3, 7), dma(3, 7), dma(3, 7), dma(3, 7),
+            dma(8), dma(8), dma(N_T), dma(N_T), pltpu.SemaphoreType.DMA, pltpu.SemaphoreType.DMA,
             dma(N_DP), dma(N_DP), dma(N_DP), dma(N_DP),
             dma(8, 3), dma(8, 3), dma(8, 3), dma(8, 3), dma(8, 3), dma(8, 3),
         ],
@@ -544,7 +561,8 @@
         out_shape=results,
         in_specs=[anywhere] * 5,
         out_specs=(anywhere,) * 5,
-        scratch_shapes=[dma(8)],
+        scratch_shapes=[pltpu.VMEM(r.shape, r.dtype) for r in results] + [dma(8), dma(8)],
+        compiler_params=pltpu.CompilerParams(vmem_limit_bytes=62 * 2**20),
         name="emit",
     )(*outs)
     return (gq, rows, key_w.T, value_w.T, query_w)

time: 333 us -> 159 us (0.48)
  Pallas kernels: 333 us -> 158 us
    pallas_call x1, Pallas kernels: 180 us -> 5.18 us  [shards(): pl.pallas_call(emit, out_shape=results, in_specs=[anywhere] * 5, out_spec...]
where the time goes in v4:
time: 159 us
  Pallas kernels  158 us (99%)
    pallas_call x1, Pallas kernels, shards(): pl.pallas_call(kernel, out_shape=results, in_specs=[in_vmem] * 5 + [anywh...  153 us
    pallas_call x1, Pallas kernels, shards(): pl.pallas_call(emit, out_shape=results, in_specs=[anywhere] * 5, out_spec...  5.18 us

profile of v4, /device:TPU:1, one launch (start us, length us, event | category | flops | bytes accessed | tf_op | source)
XLA Modules:
  0.0 158.8 jit_solution(487933060875858632)
XLA Ops:
  0.6 153.0 %grads.1 = (bf16[192,1024]{1,0:T(8,128)(2,1)}, bf16[24,16384]{1,0:T(8,128)(2,1)}, f32[64,1024]{1,0:T(8,128)}, f32[64,1024]{1,0:T(8,128)}, f32[1024,1024]{1,0:T(8,128)}) custom-call(bf16[24,16384]{1,0:T(8,128)(2,1)} %x_ref.1, bf16[64,1024]{1,0:T(8,128)(2,1)} %bitcast.4, bf16[64,1024]{1,0:T(8,128)(2,1)} %bitcast.5, s32[1,192]{1,0:T(1,128)} %seg_ref.1, ...), custom_call_target="tpu_custom_call" | custom-call | tf_op jit(solution)/shard_map/grads/pallas_call | solution.py:532
  153.7 5.2 %emit.1 = (bf16[192,1024]{1,0:T(8,128)(2,1)}, bf16[24,16384]{1,0:T(8,128)(2,1)}, f32[64,1024]{1,0:T(8,128)}, f32[64,1024]{1,0:T(8,128)}, f32[1024,1024]{1,0:T(8,128)}) custom-call(bf16[192,1024]{1,0:T(8,128)(2,1)} %get-tuple-element.15.refs_0_, bf16[24,16384]{1,0:T(8,128)(2,1)} %get-tuple-element.16.refs_1_, f32[64,1024]{1,0:T(8,128)} %get-tuple-element.17.refs_2_, ...), custom_call_target="tpu_custom_call" | custom-call | tf_op jit(solution)/shard_map/emit/pallas_call | solution.py:559

commit v5 on v4

--- a/solution.py
+++ b/solution.py
@@ -19,9 +19,10 @@
 COLS = 1024
 HD = 128
 HALF = 64
-WIDE = COLS + HD
 SLOTS = (0, 2, 6, 8, 10, 14, 4, 12)
 ORDERS = ((1, 2, 6), (2, 6, 1), (6, 1, 2))
+PARTS = ((0, 80), (80, 80), (160, 80), (240, 80), (320, 32), (352, 32))
+PART_ORDERS = ((2, 1, 6), (6, 1, 2), (1, 2, 6), (1, 6, 2), (2, 6, 1), (6, 2, 1))
 
 
 def xor_ring(place, mask):
@@ -82,9 +83,9 @@
         self.buf, self.slot_rows, self.chunks, self.orders = buf, slot_rows, chunks, orders
         self.send, self.recv, self.d, self.t = send, recv, d, t
 
-    def copies(self, stage, arriving, only=(1, 2, 0)):
+    def copies(self, stage, arriving, only=None):
         out = []
-        for c in only:
+        for c in range(len(self.chunks)) if only is None else only:
             offset, size = self.chunks[c]
             first, second, third = self.orders[c]
             held = ([0], [0, first], [0, first, second, first ^ second])[stage]
@@ -106,8 +107,8 @@
         for copy in self.copies(stage, True):
             copy.wait_recv()
 
-    def step(self, stage):
-        for c in (1, 2, 0):
+    def step(self, stage, only):
+        for c in only:
             for copy in self.copies(stage, True, (c,)):
                 copy.wait_recv()
             for copy in self.copies(stage + 1, False, (c,)):
@@ -125,9 +126,9 @@
     q_ref, do_ref, wq_ref, qw_ref,
     xg, xa, wg, kvf, kvsend, kvswap, kvrecv, heads_out, heads_in, part_out, part_in,
     cos_ref, sin_ref, mask_ref, keyp, valuep, key_ref, value_ref,
-    grads, xc, term, s1, k1, r1, s2, k2, r2, s3, k3, r3, done_out, done_in,
+    grads, owns, xc, term, s1, k1, r1, s2, k2, r2, s3, k3, r3, done_out, done_in,
     l_s, x_s, x_r, w_s, w_r, g_s, g_r, kv_s, kv_r, h_s, h_r, p_s, p_r,
-    d_s, d_r, f_s, f_r, e1_s, e1_r, e2_s, e2_r, e3_s, e3_r,
+    d_s, d_r, o_s, o_r, f_s, f_r, e1_s, e1_r, e2_s, e2_r, e3_s, e3_r,
 ):
     d = lax.axis_index("dp")
     t = lax.axis_index("tensor")
@@ -153,7 +154,7 @@
     wg[rows_at(t * HD + HALF, HALF, HALF)] = wv_ref[...]
     pl.semaphore_wait(barrier, N_DP + N_T - 2)
 
-    weights = Gather(wg, HD, ((0, 48), (48, 32), (80, 48)), ORDERS, w_s, w_r, d, t)
+    weights = Gather(wg, HD, ((0, 48), (48, 48), (96, 32)), ORDERS, w_s, w_r, d, t)
     weights.start(0)
 
     def x_copy(k):
@@ -167,8 +168,8 @@
         return carry
 
     lax.fori_loop(1, N_DP, send_x, 0)
-    weights.step(0)
-    weights.step(1)
+    weights.step(0, (1, 2, 0))
+    weights.step(1, (1, 2, 0))
     xa[d] = x_ref[:, rows_at(d * FEAT, FEAT, FEAT)]
 
     row_no = lax.broadcasted_iota(jnp.int32, (TOK, TOK), 0)
@@ -193,7 +194,7 @@
         pair = [xa[xor_dp(d, mask ^ e)].astype(F32) for e in range(2)]
         xg[rows_at(t * (N_DP * ROWS) + s * 2 * ROWS, 2 * ROWS, 16)] = jnp.concatenate(pair, axis=0).astype(BF16)
     tokens = Gather(
-        xg, N_DP * ROWS, ((0, 160), (160, 80), (240, 144)), ORDERS, g_s, g_r, d, t
+        xg, N_DP * ROWS, PARTS, PART_ORDERS, g_s, g_r, d, t
     )
     tokens.start(0)
 
@@ -219,11 +220,12 @@
     for s in range(len(SLOTS)):
         kvsend[1, s] = kv_part(2 * s + 1).astype(BF16)
     swap.start()
+    tokens.step(0, (4, 5, 0, 1))
     swap.wait()
     for s in range(1, len(SLOTS)):
         kvsend[0, s] = (kv_part(2 * s) + kvswap[s].astype(F32)).astype(BF16)
         kv_copy(s).start()
-    tokens.step(0)
+    tokens.step(0, (2, 3))
     lin = kv_part(0) + kvswap[0].astype(F32)
     for s in range(1, len(SLOTS)):
         kv_copy(s).wait()
@@ -241,6 +243,7 @@
 
     lax.fori_loop(1, N_T, send_heads, 0)
     heads_in[t] = heads_out[t // 2]
+    tokens.step(1, (0, 1, 2, 3))
 
     def wait_heads(k, carry):
         head_copy(k, lax.rem(t + k, N_T)).wait_send()
@@ -249,7 +252,6 @@
         return carry
 
     lax.fori_loop(1, N_T, wait_heads, 0)
-    tokens.step(1)
     blocks = [heads_in[i].astype(F32) for i in range(N_T)]
     first = jnp.concatenate([b[:ROWS] for b in blocks], axis=0)
     second_part = jnp.concatenate([b[ROWS:] for b in blocks], axis=0)
@@ -263,27 +265,55 @@
     for load in loads:
         load.wait()
 
-    def head_step(h, carry):
-        cols = rows_at(h * HD, HD, HD)
-        q, do = q_ref[:, cols], do_ref[:, cols]
+    def head_step(i, carry):
         key, value = key_ref[...], value_ref[...]
         allowed = mask_ref[...] > 0.0
-        weight = jnp.where(allowed, jnp.exp(dot_nt(q, key) * scale), 0.0)
-        probs = weight / jnp.sum(weight, axis=1, keepdims=True)
-        dprob = dot_nt(do, value)
-        delta = jnp.sum(probs * dprob, axis=1, keepdims=True)
-        dscore = (probs * (dprob - delta)).astype(BF16)
-        grads[0:TOK, cols] = (dot_nn(dscore, key) * scale).astype(BF16)
-        keyp[...] += dot_tn(dscore, q)
-        valuep[...] += dot_tn(probs.astype(BF16), do)
-        return carry
-
-    lax.fori_loop(0, COLS // HD, head_step, 0)
+        for_key, for_value = [], []
+        for e in range(2):
+            cols = rows_at((2 * i + e) * HD, HD, HD)
+            q, do = q_ref[:, cols], do_ref[:, cols]
+            weight = jnp.where(allowed, jnp.exp(dot_nt(q, key) * scale), 0.0)
+            probs = weight / jnp.sum(weight, axis=1, keepdims=True)
+            dprob = dot_nt(do, value)
+            delta = jnp.sum(probs * dprob, axis=1, keepdims=True)
+            dscore = (probs * (dprob - delta)).astype(BF16)
+            grads[0:TOK, cols] = (dot_nn(dscore, key) * scale).astype(BF16)
+            for_key.append(dot_tn(dscore, q))
+            for_value.append(dot_tn(probs.astype(BF16), do))
+        keyp[...] += for_key[0] + for_key[1]
+        valuep[...] += for_value[0] + for_value[1]
+        return carry
+
+    lax.fori_loop(0, 4, head_step, 0)
+    place = {}
+    for s, mask in enumerate(SLOTS):
+        place[mask], place[mask ^ 1] = 2 * s, 2 * s + 1
+
+    def block_of(buf, mask):
+        return buf.at[pl.ds(place[mask] * TOK, TOK)]
+
+    def grad_copy(buf, mask, link):
+        there = mask ^ link
+        n = place[there]
+        send, recv = (d_s, d_r) if buf is grads else (o_s, o_r)
+        return remote(block_of(buf, mask), block_of(buf, there), send.at[n], recv.at[n], xor_dp(d, link), t)
+
+    def grad_arrival(buf, mask):
+        n = place[mask]
+        send, recv = (d_s, d_r) if buf is grads else (o_s, o_r)
+        return remote(block_of(buf, mask), block_of(buf, mask), send.at[n], recv.at[n], xor_dp(d, 1), t)
+
+    onward = {8: (2, 6, 1), 2: (1,), 6: (1,), 10: (1,), 14: (2, 1), 4: (1,), 12: (1,)}
+
     key_part = keyp[...] * scale
     part_out[0:TOK] = key_part.astype(BF16)
     part_out[TOK : 2 * TOK] = valuep[...].astype(BF16)
     part = remote(part_out, part_in, p_s, p_r, d, xor_t(t, 1))
     part.start()
+    for link in (8, 2, 6, 1):
+        grad_copy(grads, 0, link).start()
+    gq_out = pltpu.make_async_copy(grads.at[0:TOK], gq_hbm, l_s.at[3])
+    gq_out.start()
     part.wait()
     key_rot = key_part + part_in[0:TOK].astype(F32)
     value_sum = valuep[...] + part_in[TOK : 2 * TOK].astype(F32)
@@ -291,45 +321,25 @@
     is_first = lax.rem(t, 2) == 0
     own_key = jnp.where(is_first, upper * cosine + lower * sine, lower * cosine - upper * sine)
     own_value = jnp.where(is_first, value_sum[:, :HALF], value_sum[:, HALF:])
-    grads[0:TOK, COLS:WIDE] = jnp.concatenate([own_key, own_value], axis=1).astype(BF16)
-
-    place = {}
-    for s, mask in enumerate(SLOTS):
-        place[mask], place[mask ^ 1] = 2 * s, 2 * s + 1
-
-    def block_of(mask):
-        return grads.at[pl.ds(place[mask] * TOK, TOK)]
-
-    def grad_copy(mask, link):
-        there = mask ^ link
-        return remote(
-            block_of(mask), block_of(there), d_s.at[place[there]], d_r.at[place[there]], xor_dp(d, link), t
-        )
-
-    def grad_arrival(mask):
-        n = place[mask]
-        return remote(block_of(mask), block_of(mask), d_s.at[n], d_r.at[n], xor_dp(d, 1), t)
-
+    owns[0:TOK] = jnp.concatenate([own_key, own_value], axis=1).astype(BF16)
     for link in (8, 2, 6, 1):
-        grad_copy(0, link).start()
-    gq_out = pltpu.make_async_copy(grads.at[0:TOK, 0:COLS], gq_hbm, l_s.at[3])
-    gq_out.start()
-    onward = {8: (2, 6, 1), 2: (1,), 6: (1,), 10: (1,), 14: (2, 1), 4: (1,), 12: (1,)}
+        grad_copy(owns, 0, link).start()
 
     def receive(*masks):
         for mask in masks:
-            grad_arrival(mask).wait_recv()
-            for link in onward.get(mask, ()):
-                grad_copy(mask, link).start()
-            if mask == 14:
-                grad_copy(2, 6).start()
+            for buf in (grads, owns):
+                grad_arrival(buf, mask).wait_recv()
+                for link in onward.get(mask, ()):
+                    grad_copy(buf, mask, link).start()
+                if mask == 14:
+                    grad_copy(buf, 2, 6).start()
 
     def multiply(s):
         def part(n, carry):
             cols = rows_at(n * 256, 256, 256)
-            own = grads[s * 2 * TOK : (s + 1) * 2 * TOK]
-            total = dot_nt(own[:, :COLS], wq_ref[rows_at(n * 256, 256, 256)])
-            term[:, cols] = total + dot_nn(own[:, COLS:], wg[rows_at(t * HD, HD, HD), cols])
+            rows = slice(s * 2 * TOK, (s + 1) * 2 * TOK)
+            total = dot_nt(grads[rows], wq_ref[rows_at(n * 256, 256, 256)])
+            term[:, cols] = total + dot_nn(owns[rows], wg[rows_at(t * HD, HD, HD), cols])
             return carry
 
         lax.fori_loop(0, 4, part, 0)
@@ -405,23 +415,34 @@
     def weight_part(n, part):
         cols = slice(n * 256, (n + 1) * 256)
         rows = slice(part * deep, (part + 1) * deep)
-        total = dot_tn(xc[rows, cols], grads[rows, :COLS])
+        total = dot_tn(xc[rows, cols], grads[rows])
         if part == 0:
             qw_ref[cols] = total
         else:
             qw_ref[cols] += total
             weight_copy(n).start()
 
+    def own_rows(*steps):
+        for s in steps:
+            for e in range(2):
+                n, mask = 2 * s + e, SLOTS[s] ^ e
+                if n:
+                    final_copy(n, mask).wait_recv()
+                cols = rows_at(xor_dp(d, mask) * FEAT, FEAT, FEAT)
+                gr_ref[:, cols] = unfold(done_in[n].astype(F32)).astype(BF16)
+
     def pair_weights(n, carry):
         cols = rows_at(n * 256, 256, 256)
-        total = dot_tn(grads[:, COLS:], xc[:, cols])
+        total = dot_tn(owns[...], xc[:, cols])
         kw_ref[:, cols] = total[:HALF]
         vw_ref[:, cols] = total[HALF:]
         return carry
 
     receive(1)
     begin(0)
-    receive(8, 2, 6)
+    receive(8)
+    tokens.step(1, (4, 5))
+    receive(2, 6)
     second(0)
     receive(3)
     begin(1)
@@ -465,22 +486,23 @@
     weight_part(1, 0)
     third(6)
     weight_part(1, 1)
+    weight_part(2, 0)
     third(7)
     last(6)
-    weight_part(2, 0)
     weight_part(2, 1)
+    lax.fori_loop(0, 4, pair_weights, 0)
+    own_rows(0, 1, 2, 3, 4)
     last(7)
     weight_part(3, 0)
+    own_rows(5)
     weight_part(3, 1)
-    lax.fori_loop(0, 4, pair_weights, 0)
+    own_rows(6, 7)
     for s, base in enumerate(SLOTS):
         for e in range(2):
-            n, mask = 2 * s + e, base ^ e
-            if n:
-                final_copy(n, mask).wait()
-            gr_ref[:, rows_at(xor_dp(d, mask) * FEAT, FEAT, FEAT)] = unfold(done_in[n].astype(F32)).astype(BF16)
-            if n:
-                grad_arrival(mask).wait_send()
+            if 2 * s + e:
+                final_copy(2 * s + e, base ^ e).wait_send()
+                grad_arrival(grads, base ^ e).wait_send()
+                grad_arrival(owns, base ^ e).wait_send()
         for o in range(3):
             for stage in range(3):
                 hop(s, o, stage).wait_send()
@@ -541,14 +563,14 @@
             vmem(4, 48, HD), vmem(N_T, 48, HD), vmem(2 * TOK, HD), vmem(2 * TOK, HD),
             vmem(TOK, HALF, dtype=F32), vmem(TOK, HALF, dtype=F32), vmem(TOK, TOK, dtype=F32),
             vmem(TOK, HD, dtype=F32), vmem(TOK, HD, dtype=F32), vmem(TOK, HD), vmem(TOK, HD),
-            vmem(N_DP * TOK, WIDE), vmem(N_DP * TOK, FEAT), vmem(2 * TOK, FEAT, dtype=F32),
+            vmem(N_DP * TOK, COLS), vmem(N_DP * TOK, HD), vmem(N_DP * TOK, FEAT), vmem(2 * TOK, FEAT, dtype=F32),
             vmem(8, 3, 128, 512), vmem(8, 3, 128, 512), vmem(8, 3, 128, 512),
             vmem(8, 3, 64, 512), vmem(8, 3, 64, 512), vmem(8, 3, 64, 512),
             vmem(8, 3, 32, 512), vmem(8, 3, 32, 512, dtype=F32), vmem(8, 3, 32, 512),
             vmem(N_DP, 48, 512), vmem(N_DP, 48, 512),
-            dma(8), dma(N_DP), dma(N_DP), dma(3, 7), dma(3, 7), dma(3, 7), dma(3, 7),
+            dma(8), dma(N_DP), dma(N_DP), dma(3, 7), dma(3, 7), dma(6, 7), dma(6, 7),
             dma(8), dma(8), dma(N_T), dma(N_T), pltpu.SemaphoreType.DMA, pltpu.SemaphoreType.DMA,
-            dma(N_DP), dma(N_DP), dma(N_DP), dma(N_DP),
+            dma(N_DP), dma(N_DP), dma(N_DP), dma(N_DP), dma(N_DP), dma(N_DP),
             dma(8, 3), dma(8, 3), dma(8, 3), dma(8, 3), dma(8, 3), dma(8, 3),
         ],
         compiler_params=pltpu.CompilerParams(

time: 159 us -> 157 us (0.987)
  Pallas kernels: 158 us -> 156 us
    pallas_call x1, Pallas kernels: 153 us -> 151 us  [shards(): pl.pallas_call(kernel, out_shape=results, in_specs=[in_vmem] * 5 + [anywh...]
where the time goes in v5:
time: 157 us
  Pallas kernels  156 us (99%)
    pallas_call x1, Pallas kernels, shards(): pl.pallas_call(kernel, out_shape=results, in_specs=[in_vmem] * 5 + [anywh...  151 us
    pallas_call x1, Pallas kernels, shards(): pl.pallas_call(emit, out_shape=results, in_specs=[anywhere] * 5, out_spec...  5.18 us

profile of v5, /device:TPU:1, one launch (start us, length us, event | category | flops | bytes accessed | tf_op | source)
XLA Modules:
  0.0 157.1 jit_solution(15047688381480309463)
XLA Ops:
  0.6 151.2 %grads.1 = (bf16[192,1024]{1,0:T(8,128)(2,1)}, bf16[24,16384]{1,0:T(8,128)(2,1)}, f32[64,1024]{1,0:T(8,128)}, f32[64,1024]{1,0:T(8,128)}, f32[1024,1024]{1,0:T(8,128)}) custom-call(bf16[24,16384]{1,0:T(8,128)(2,1)} %x_ref.1, bf16[64,1024]{1,0:T(8,128)(2,1)} %bitcast.4, bf16[64,1024]{1,0:T(8,128)(2,1)} %bitcast.5, s32[1,192]{1,0:T(1,128)} %seg_ref.1, ...), custom_call_target="tpu_custom_call" | custom-call | tf_op jit(solution)/shard_map/grads/pallas_call | solution.py:554
  151.8 5.2 %emit.1 = (bf16[192,1024]{1,0:T(8,128)(2,1)}, bf16[24,16384]{1,0:T(8,128)(2,1)}, f32[64,1024]{1,0:T(8,128)}, f32[64,1024]{1,0:T(8,128)}, f32[1024,1024]{1,0:T(8,128)}) custom-call(bf16[192,1024]{1,0:T(8,128)(2,1)} %get-tuple-element.15.refs_0_, bf16[24,16384]{1,0:T(8,128)(2,1)} %get-tuple-element.16.refs_1_, f32[64,1024]{1,0:T(8,128)} %get-tuple-element.17.refs_2_, ...), custom_call_target="tpu_custom_call" | custom-call | tf_op jit(solution)/shard_map/emit/pallas_call | solution.py:581

commit v6 on v5

--- a/solution.py
+++ b/solution.py
@@ -421,15 +421,6 @@
         else:
             qw_ref[cols] += total
             weight_copy(n).start()
-
-    def own_rows(*steps):
-        for s in steps:
-            for e in range(2):
-                n, mask = 2 * s + e, SLOTS[s] ^ e
-                if n:
-                    final_copy(n, mask).wait_recv()
-                cols = rows_at(xor_dp(d, mask) * FEAT, FEAT, FEAT)
-                gr_ref[:, cols] = unfold(done_in[n].astype(F32)).astype(BF16)
 
     def pair_weights(n, carry):
         cols = rows_at(n * 256, 256, 256)
@@ -486,23 +477,23 @@
     weight_part(1, 0)
     third(6)
     weight_part(1, 1)
-    weight_part(2, 0)
     third(7)
     last(6)
+    weight_part(2, 0)
     weight_part(2, 1)
-    lax.fori_loop(0, 4, pair_weights, 0)
-    own_rows(0, 1, 2, 3, 4)
     last(7)
     weight_part(3, 0)
-    own_rows(5)
     weight_part(3, 1)
-    own_rows(6, 7)
+    lax.fori_loop(0, 4, pair_weights, 0)
     for s, base in enumerate(SLOTS):
         for e in range(2):
-            if 2 * s + e:
-                final_copy(2 * s + e, base ^ e).wait_send()
-                grad_arrival(grads, base ^ e).wait_send()
-                grad_arrival(owns, base ^ e).wait_send()
+            n, mask = 2 * s + e, base ^ e
+            if n:
+                final_copy(n, mask).wait()
+            gr_ref[:, rows_at(xor_dp(d, mask) * FEAT, FEAT, FEAT)] = unfold(done_in[n].astype(F32)).astype(BF16)
+            if n:
+                grad_arrival(grads, mask).wait_send()
+                grad_arrival(owns, mask).wait_send()
         for o in range(3):
             for stage in range(3):
                 hop(s, o, stage).wait_send()

time: 157 us -> 156 us (level)
  no operation moved by 1% of the time
where the time goes in v6:
time: 156 us
  Pallas kernels  155 us (99%)
    pallas_call x1, Pallas kernels, shards(): pl.pallas_call(kernel, out_shape=results, in_specs=[in_vmem] * 5 + [anywh...  150 us
    pallas_call x1, Pallas kernels, shards(): pl.pallas_call(emit, out_shape=results, in_specs=[anywhere] * 5, out_spec...  5.18 us

profile of v6, /device:TPU:1, one launch (start us, length us, event | category | flops | bytes accessed | tf_op | source)
XLA Modules:
  0.0 155.8 jit_solution(6119561109293834040)
XLA Ops:
  0.6 149.8 %grads.1 = (bf16[192,1024]{1,0:T(8,128)(2,1)}, bf16[24,16384]{1,0:T(8,128)(2,1)}, f32[64,1024]{1,0:T(8,128)}, f32[64,1024]{1,0:T(8,128)}, f32[1024,1024]{1,0:T(8,128)}) custom-call(bf16[24,16384]{1,0:T(8,128)(2,1)} %x_ref.1, bf16[64,1024]{1,0:T(8,128)(2,1)} %bitcast.4, bf16[64,1024]{1,0:T(8,128)(2,1)} %bitcast.5, s32[1,192]{1,0:T(1,128)} %seg_ref.1, ...), custom_call_target="tpu_custom_call" | custom-call | tf_op jit(solution)/shard_map/grads/pallas_call | solution.py:545
  150.4 5.2 %emit.1 = (bf16[192,1024]{1,0:T(8,128)(2,1)}, bf16[24,16384]{1,0:T(8,128)(2,1)}, f32[64,1024]{1,0:T(8,128)}, f32[64,1024]{1,0:T(8,128)}, f32[1024,1024]{1,0:T(8,128)}) custom-call(bf16[192,1024]{1,0:T(8,128)(2,1)} %get-tuple-element.15.refs_0_, bf16[24,16384]{1,0:T(8,128)(2,1)} %get-tuple-element.16.refs_1_, f32[64,1024]{1,0:T(8,128)} %get-tuple-element.17.refs_2_, ...), custom_call_target="tpu_custom_call" | custom-call | tf_op jit(solution)/shard_map/emit/pallas_call | solution.py:572
